TPU v7x, 512 devices: a whole 4x4x16 slice. The times are simulated.
512 devices in a mesh: mem: 8 (over y, core), gy: 4 (over z_hi), gx: 16 (over x, z_lo).
Axes of the slice: x: 4, y: 4, z: 16 (z_hi: 4, z_lo: 4; z = z_hi * 4 + z_lo), core: 2. Of those that a mesh axis runs over, the one named last changes fastest.
Arguments:
- perturbations: bfloat16 [16, 5, 16, 32, 2048], P('mem', None, None, 'gy', 'gx'), may hold values from -6 to 6
- control: float32 [16, 16, 32, 2048], P('mem', None, 'gy', 'gx'), may hold values from -6 to 6
- background: float32 [5, 16, 32, 2048], P(None, 'mem', 'gy', 'gx'), may hold values from -6 to 6
- obs_cell: int32 [128, 2048], P('gy', 'gx'), may hold values from 0 to 81919
- huber_flag: int32 [128, 2048], P('gy', 'gx'), may hold values 0 or 1
- innovation: float32 [128, 2048], P('gy', 'gx'), may hold values from -6 to 6
- precision: float32 [128, 2048], P('gy', 'gx'), may hold values from 10 to 100
Outputs:
- analysis: float32 [5, 16, 32, 2048], P(None, 'mem', 'gy', 'gx')
- control_out: float32 [16, 16, 32, 2048], P('mem', None, 'gy', 'gx')
Inputs may be any that keep to these rules, and one draw needn't show every extreme that they name: `obs_cell`: a cell of its tile, ordered by variable, then level, then row, then column.
All inputs are finite; a program needn't handle non-finite values. No bound on the sum of `huber_flag` on one device may be relied on, other than what follows from the above.
Results may differ from a plain program's by a relative error of at most 0.0003.
Values sent between devices are 32-bit elements; how exact they have to be, the bound alone decides.
A program may use at most 64 MiB of HBM per device.

v0:
```python
import jax
import jax.numpy as jnp
from jax import lax
from jax.sharding import PartitionSpec as P

ITERS = 2


huber_width = 1.0


def extended(value, sides, width):
    for axis, dim in sides:
        peers, length = (lax.axis_size(axis), value.shape[dim])
        up = [(i, (i + 1) % peers) for i in range(peers - 1)]
        down = [(j, i) for i, j in up]
        last = lax.slice_in_dim(value, length - width, length, axis=dim)
        initial = lax.slice_in_dim(value, 0, width, axis=dim)
        before = lax.ppermute(last, axis, up)
        after = lax.ppermute(initial, axis, down)
        value = jnp.concatenate([before, value, after], axis=dim)
    return value


def filter_taps():
    offsets = jnp.arange(-4, 5).astype(jnp.float32)
    raw = jnp.exp(-offsets * offsets / 8.0)
    return raw / jnp.sum(raw)


def smooth(field):
    weights = filter_taps()
    rows, cols = (field.shape[2], field.shape[3])
    padded = extended(field, (("gy", 2), ("gx", 3)), 4)
    along = sum((weights[offset] * padded[..., :, offset : offset + cols] for offset in range(9)))
    return sum((weights[offset] * along[..., offset : offset + rows, :] for offset in range(9)))


def member_sum(perturbations, alpha):
    return jnp.sum(perturbations.astype(jnp.float32) * alpha[:, None], axis=0)


def project(perturbations, adjoint):
    return jnp.sum(perturbations.astype(jnp.float32) * adjoint[None], axis=1)


def step_size(grad_local, grad_total, curv_local):
    grad_total, curv_total = lax.psum((grad_local, curv_local), ("mem", "gy", "gx"))
    return grad_total / (grad_total + curv_total)


def robust_weight(misfit, flagged):
    scaled = misfit / huber_width
    return jnp.where(flagged, 1.0 / jnp.sqrt(1.0 + scaled * scaled), 1.0)


def per_device(perturbations, control, background, obs_cell, huber_flag, innovation, precision):
    levels = perturbations.shape[2]
    share = levels // lax.axis_size("mem")
    first = lax.axis_index("mem") * share
    flat_cell = obs_cell.reshape(-1)
    observed = innovation.reshape(-1)
    inverse_var = precision.reshape(-1)
    flagged = huber_flag.reshape(-1) == 1
    state = control
    smoothed = smooth(state)
    partial_value = member_sum(perturbations, smoothed)
    increment = lax.psum(partial_value, "mem")
    inside = jnp.ones(flat_cell.shape, bool)
    counted = inside & (lax.axis_index("mem") == 0)
    for iteration in range(ITERS):
        misfit = jnp.where(inside, increment.reshape(-1)[flat_cell] - observed, 0.0)
        weight = robust_weight(misfit, flagged)
        weighted = jnp.where(inside, inverse_var * weight * misfit, 0.0)
        adjoint_part = (
            jnp.zeros((increment.size,), jnp.float32)
            .at[flat_cell]
            .add(weighted)
            .reshape(increment.shape)
        )
        grad = state + smooth(project(perturbations, adjoint_part))
        grad_local = jnp.sum(grad * grad)
        delta_part = member_sum(perturbations, smooth(grad))
        delta = lax.psum(delta_part, "mem")
        seen_step = delta.reshape(-1)[flat_cell]
        curv_local = jnp.sum(jnp.where(counted, inverse_var * weight * seen_step * seen_step, 0.0))
        step = step_size(grad_local, grad_local, curv_local)
        state = state - step * grad
        increment = increment - step * delta
    mine = lax.dynamic_slice_in_dim(increment, first, share, 1)
    return (background + mine, state)


def solution(mesh):
    in_specs = (
        P("mem", None, None, "gy", "gx"),
        P("mem", None, "gy", "gx"),
        P(None, "mem", "gy", "gx"),
        P("gy", "gx"),
        P("gy", "gx"),
        P("gy", "gx"),
        P("gy", "gx"),
    )
    out_specs = (P(None, "mem", "gy", "gx"), P("mem", None, "gy", "gx"))
    return jax.shard_map(
        per_device, mesh=mesh, in_specs=in_specs, out_specs=out_specs, check_vma=False
    )
```

profile of v0, /device:TPU:1, one launch (start us, length us, event | category | flops | bytes accessed | tf_op | source)
XLA Modules:
  0.0 819.3 jit_solution(18394527784366242883)
XLA Ops:
  8.2 9.6 %collective-permute-start = (f32[2,16,4,128]{3,2,1,0:T(4,128)S(1)}, f32[2,16,4,128]{3,2,1,0:T(4,128)S(1)}, u32[]{:S(2)}, u32[]{:S(2)}) collective-permute-start(f32[2,16,4,128]{3,2,1,0:T(4,128)S(1)} %get-tuple-element.40), channel_id=1, source_target_pairs={{0,16},{16,32},{32,48},{1,17},{17,33},{33,49},{2,18},{18,34},{34,5... | collective-permute-start | bytes 196616 | tf_op jit(solution)/shard_map/ppermute | solution.py:19
  20.5 12.5 %collective-permute-done.1 = f32[2,16,4,128]{3,2,1,0:T(4,128)S(1)} collective-permute-done((f32[2,16,4,128]{3,2,1,0:T(4,128)S(1)}, f32[2,16,4,128]{3,2,1,0:T(4,128)S(1)}, u32[]{:S(2)}, u32[]{:S(2)}) %collective-permute-start.1) | collective-permute-done | bytes 65568 | tf_op jit(solution)/shard_map/ppermute | solution.py:20
  39.4 9.4 %collective-permute-done.3 = f32[2,16,16,4]{3,2,1,0:T(8,128)S(1)} collective-permute-done((f32[2,16,16,4]{3,2,1,0:T(8,128)S(1)}, f32[2,16,16,4]{3,2,1,0:T(8,128)S(1)}, u32[]{:S(2)}, u32[]{:S(2)}) %collective-permute-start.3) | collective-permute-done | bytes 8224 | tf_op jit(solution)/shard_map/ppermute | solution.py:20
  49.2 6.2 fusion.37
  55.5 5.9 fusion.83
  62.3 74.1 %all-reduce.6.cloned.1.call-done = f32[5,16,8,128]{3,2,1,0:T(8,128)} async-done(((f32[5,16,8,128]{3,2,1,0:T(8,128)}), f32[5,16,8,128]{3,2,1,0:T(8,128)}) %all-reduce.6.cloned.1.call-update) | async-done | bytes 327696 | tf_op jit(solution)/shard_map/psum | solution.py:68
  136.4 19.6 %gather_fusion = f32[4096]{0:T(1024)S(1)} fusion(f32[81920]{0:T(1024)} %bitcast.67, s32[4096]{0:T(1024)S(1)} %broadcast_clamp_fusion), kind=kCustom, calls=%fused_computation | custom fusion | bytes 49152 | tf_op jit(solution)/shard_map/gather | solution.py:72
  156.0 22.0 %scatter_custom_fusion = f32[81920]{0:T(1024)S(1)} fusion(s32[4096]{0:T(1024)S(1)} %bitcast.73, f32[4096]{0:T(1024)S(1)} %get-tuple-element.10, f32[]{:T(128)} %constant.13.clone.1), kind=kCustom, calls=%fused_computation.114 | custom fusion | flops 4096 | bytes 327684 | tf_op jit(solution)/shard_map/scatter-add | solution.py:78
  178.1 6.8 collective-permute-start.4
  186.2 7.7 collective-permute-done.5
  200.5 9.8 %collective-permute-done.7 = f32[2,16,16,4]{3,2,1,0:T(8,128)S(1)} collective-permute-done((f32[2,16,16,4]{3,2,1,0:T(8,128)S(1)}, f32[2,16,16,4]{3,2,1,0:T(8,128)S(1)}, u32[]{:S(2)}, u32[]{:S(2)}) %collective-permute-start.7) | collective-permute-done | bytes 8224 | tf_op jit(solution)/shard_map/ppermute | solution.py:20
  210.6 6.2 fusion.29
  216.9 6.4 multiply_reduce_fusion.1
  223.3 6.8 collective-permute-start.8
  231.5 8.7 %collective-permute-done.9 = f32[2,16,4,128]{3,2,1,0:T(4,128)S(1)} collective-permute-done((f32[2,16,4,128]{3,2,1,0:T(4,128)S(1)}, f32[2,16,4,128]{3,2,1,0:T(4,128)S(1)}, u32[]{:S(2)}, u32[]{:S(2)}) %collective-permute-start.9) | collective-permute-done | bytes 65568 | tf_op jit(solution)/shard_map/ppermute | solution.py:20
  245.2 6.6 collective-permute-done.11
  252.2 6.2 fusion.21
  265.1 81.1 %all-reduce.8.cloned.1.call-done = f32[5,16,8,128]{3,2,1,0:T(8,128)} async-done(((f32[5,16,8,128]{3,2,1,0:T(8,128)}), f32[5,16,8,128]{3,2,1,0:T(8,128)}) %all-reduce.8.cloned.1.call-update) | async-done | bytes 327696 | tf_op jit(solution)/shard_map/psum | solution.py:84
  346.2 19.6 %gather_fusion.1 = f32[4096]{0:T(1024)S(1)} fusion(f32[81920]{0:T(1024)} %bitcast.68, s32[4096]{0:T(1024)S(1)} %broadcast_clamp_fusion), kind=kCustom, calls=%fused_computation.1 | custom fusion | bytes 49152 | tf_op jit(solution)/shard_map/gather | solution.py:85
  366.5 106.0 %all-reduce.1 = (f32[]{:T(128)}, f32[]{:T(128)}) all-reduce(f32[]{:T(128)} %get-tuple-element.8, f32[]{:T(128)} %fusion.93), channel_id=1, replica_groups=mesh['mem'=8,'gy'=4,'gx'=16] {'mem','gy','gx'}, use_global_device_ids=true, to_apply=%region_6.7 | all-reduce | flops 2 | bytes 16 | tf_op jit(solution)/shard_map/psum | solution.py:48
  474.3 23.0 %gather_fusion.2 = f32[4096]{0:T(1024)S(1)} fusion(f32[81920]{0:T(1024)S(1)} %bitcast.66, s32[4096]{0:T(1024)S(1)} %broadcast_clamp_fusion), kind=kCustom, calls=%fused_computation.2 | custom fusion | bytes 49152 | tf_op jit(solution)/shard_map/gather | solution.py:72
  497.4 22.0 %scatter_custom_fusion.1 = f32[81920]{0:T(1024)S(1)} fusion(s32[4096]{0:T(1024)S(1)} %bitcast.74, f32[4096]{0:T(1024)S(1)} %fusion.107, f32[]{:T(128)} %constant.13.clone.1), kind=kCustom, calls=%fused_computation.112 | custom fusion | flops 4096 | bytes 327684 | tf_op jit(solution)/shard_map/scatter-add | solution.py:78
  524.9 7.6 collective-permute-done.13
  540.4 11.5 %collective-permute-done.15 = f32[2,16,16,4]{3,2,1,0:T(8,128)S(1)} collective-permute-done((f32[2,16,16,4]{3,2,1,0:T(8,128)S(1)}, f32[2,16,16,4]{3,2,1,0:T(8,128)S(1)}, u32[]{:S(2)}, u32[]{:S(2)}) %collective-permute-start.15) | collective-permute-done | bytes 8224 | tf_op jit(solution)/shard_map/ppermute | solution.py:20
  552.3 6.2 fusion.13
  558.6 6.4 multiply_reduce_fusion
  572.0 11.6 %collective-permute-done.17 = f32[2,16,4,128]{3,2,1,0:T(4,128)S(1)} collective-permute-done((f32[2,16,4,128]{3,2,1,0:T(4,128)S(1)}, f32[2,16,4,128]{3,2,1,0:T(4,128)S(1)}, u32[]{:S(2)}, u32[]{:S(2)}) %collective-permute-start.17) | collective-permute-done | bytes 65568 | tf_op jit(solution)/shard_map/ppermute | solution.py:20
  590.6 6.7 collective-permute-done.19
  597.7 6.2 fusion.5
  610.6 71.8 %all-reduce.10.cloned.1.call-done = f32[5,16,8,128]{3,2,1,0:T(8,128)} async-done(((f32[5,16,8,128]{3,2,1,0:T(8,128)}), f32[5,16,8,128]{3,2,1,0:T(8,128)}) %all-reduce.10.cloned.1.call-update) | async-done | bytes 327696 | tf_op jit(solution)/shard_map/psum | solution.py:84
  682.4 19.5 %gather_fusion.3 = f32[4096]{0:T(1024)S(1)} fusion(f32[81920]{0:T(1024)} %bitcast.69, s32[4096]{0:T(1024)S(1)} %broadcast_clamp_fusion), kind=kCustom, calls=%fused_computation.3 | custom fusion | bytes 49152 | tf_op jit(solution)/shard_map/gather | solution.py:85
  702.6 106.0 %all-reduce = (f32[]{:T(128)}, f32[]{:T(128)}) all-reduce(f32[]{:T(128)} %get-tuple-element.6, f32[]{:T(128)} %fusion.95), channel_id=1, replica_groups=mesh['mem'=8,'gy'=4,'gx'=16] {'mem','gy','gx'}, use_global_device_ids=true, to_apply=%region_14.15 | all-reduce | flops 2 | bytes 16 | tf_op jit(solution)/shard_map/psum | solution.py:48
  (90 shorter events, 71.1 us)
Async XLA Ops:
  7.2 25.8 %copy-start.3 = (f32[2,16,8,128]{3,2,1,0:T(8,128)S(1)}, f32[2,16,8,128]{3,2,1,0:T(8,128)}, u32[]{:S(2)}) copy-start(f32[2,16,8,128]{3,2,1,0:T(8,128)} %param.8) | copy-start | bytes 393220
  7.2 129.2 %all-reduce.6.cloned.1.call-start = ((), (), s32[]{:S(2)}) async-start(), calls=%async_computation | async-start | bytes 655360 | tf_op jit(solution)/shard_map/psum | solution.py:68
  7.2 12.6 %copy-start.7 = (s32[32,128]{1,0:T(8,128)S(1)}, s32[32,128]{1,0:T(8,128)}, u32[]{:S(2)}) copy-start(s32[32,128]{1,0:T(8,128)} %param.10) | copy-start | bytes 49156
  8.2 12.3 %collective-permute-start = (f32[2,16,4,128]{3,2,1,0:T(4,128)S(1)}, f32[2,16,4,128]{3,2,1,0:T(4,128)S(1)}, u32[]{:S(2)}, u32[]{:S(2)}) collective-permute-start(f32[2,16,4,128]{3,2,1,0:T(4,128)S(1)} %get-tuple-element.40), channel_id=1, source_target_pairs={{0,16},{16,32},{32,48},{1,17},{17,33},{33,49},{2,18},{18,34},{34,5... | collective-permute-start | bytes 196616 | tf_op jit(solution)/shard_map/ppermute | solution.py:19
  17.9 15.1 %collective-permute-start.1 = (f32[2,16,4,128]{3,2,1,0:T(4,128)S(1)}, f32[2,16,4,128]{3,2,1,0:T(4,128)S(1)}, u32[]{:S(2)}, u32[]{:S(2)}) collective-permute-start(f32[2,16,4,128]{3,2,1,0:T(4,128)S(1)} %get-tuple-element.41), channel_id=1, source_target_pairs={{16,0},{32,16},{48,32},{17,1},{33,17},{49,33},{18,2},{34,18},{50,3... | collective-permute-start | bytes 196616 | tf_op jit(solution)/shard_map/ppermute | solution.py:20
  33.2 6.2 collective-permute-start.2
  34.5 14.4 %collective-permute-start.3 = (f32[2,16,16,4]{3,2,1,0:T(8,128)S(1)}, f32[2,16,16,4]{3,2,1,0:T(8,128)S(1)}, u32[]{:S(2)}, u32[]{:S(2)}) collective-permute-start(f32[2,16,16,4]{3,2,1,0:T(8,128)S(1)} %get-tuple-element.31), channel_id=1, source_target_pairs={{1,0},{2,1},{3,2},{4,3},{5,4},{6,5},{7,6},{8,7},{9,8},{10,9},{11,1... | collective-permute-start | bytes 24584 | tf_op jit(solution)/shard_map/ppermute | solution.py:20
  55.5 5.9 copy-start.2
  62.2 284.0 %all-reduce.8.cloned.1.call-start = ((), (), s32[]{:S(2)}) async-start(), calls=%async_computation.1 | async-start | bytes 655360 | tf_op jit(solution)/shard_map/psum | solution.py:84
  136.4 19.6 %copy-start.4 = (f32[32,128]{1,0:T(8,128)S(1)}, f32[32,128]{1,0:T(8,128)}, u32[]{:S(2)}) copy-start(f32[32,128]{1,0:T(8,128)} %param.13) | copy-start | bytes 49156
  136.4 19.6 %copy-start.5 = (f32[32,128]{1,0:T(8,128)S(1)}, f32[32,128]{1,0:T(8,128)}, u32[]{:S(2)}) copy-start(f32[32,128]{1,0:T(8,128)} %param.12) | copy-start | bytes 49156
  136.4 19.6 %copy-start.8 = (s32[32,128]{1,0:T(8,128)S(1)}, s32[32,128]{1,0:T(8,128)}, u32[]{:S(2)}) copy-start(s32[32,128]{1,0:T(8,128)} %param.11) | copy-start | bytes 49156
  178.1 8.1 collective-permute-start.4
  184.9 9.0 %collective-permute-start.5 = (f32[2,16,4,128]{3,2,1,0:T(4,128)S(1)}, f32[2,16,4,128]{3,2,1,0:T(4,128)S(1)}, u32[]{:S(2)}, u32[]{:S(2)}) collective-permute-start(f32[2,16,4,128]{3,2,1,0:T(4,128)S(1)} %get-tuple-element.39), channel_id=1, source_target_pairs={{16,0},{32,16},{48,32},{17,1},{33,17},{49,33},{18,2},{34,18},{50,3... | collective-permute-start | bytes 196616 | tf_op jit(solution)/shard_map/ppermute | solution.py:20
  194.1 6.4 collective-permute-start.6
  197.2 13.1 %collective-permute-start.7 = (f32[2,16,16,4]{3,2,1,0:T(8,128)S(1)}, f32[2,16,16,4]{3,2,1,0:T(8,128)S(1)}, u32[]{:S(2)}, u32[]{:S(2)}) collective-permute-start(f32[2,16,16,4]{3,2,1,0:T(8,128)S(1)} %get-tuple-element.27), channel_id=1, source_target_pairs={{1,0},{2,1},{3,2},{4,3},{5,4},{6,5},{7,6},{8,7},{9,8},{10,9},{11,1... | collective-permute-start | bytes 24584 | tf_op jit(solution)/shard_map/ppermute | solution.py:20
  223.3 8.1 collective-permute-start.8
  230.2 10.0 %collective-permute-start.9 = (f32[2,16,4,128]{3,2,1,0:T(4,128)S(1)}, f32[2,16,4,128]{3,2,1,0:T(4,128)S(1)}, u32[]{:S(2)}, u32[]{:S(2)}) collective-permute-start(f32[2,16,4,128]{3,2,1,0:T(4,128)S(1)} %get-tuple-element.37), channel_id=1, source_target_pairs={{16,0},{32,16},{48,32},{17,1},{33,17},{49,33},{18,2},{34,18},{50,3... | collective-permute-start | bytes 196616 | tf_op jit(solution)/shard_map/ppermute | solution.py:20
  240.4 4.8 collective-permute-start.10
  241.9 9.9 %collective-permute-start.11 = (f32[2,16,16,4]{3,2,1,0:T(8,128)S(1)}, f32[2,16,16,4]{3,2,1,0:T(8,128)S(1)}, u32[]{:S(2)}, u32[]{:S(2)}) collective-permute-start(f32[2,16,16,4]{3,2,1,0:T(8,128)S(1)} %get-tuple-element.23), channel_id=1, source_target_pairs={{1,0},{2,1},{3,2},{4,3},{5,4},{6,5},{7,6},{8,7},{9,8},{10,9},{11,1... | collective-permute-start | bytes 24584 | tf_op jit(solution)/shard_map/ppermute | solution.py:20
  265.1 417.3 %all-reduce.10.cloned.1.call-start = ((), (), s32[]{:S(2)}) async-start(), calls=%async_computation.2 | async-start | bytes 655360 | tf_op jit(solution)/shard_map/psum | solution.py:84
  346.2 128.0 %copy-start = (f32[5,16,8,128]{3,2,1,0:T(8,128)S(1)}, f32[5,16,8,128]{3,2,1,0:T(8,128)}, u32[]{:S(2)}) copy-start(f32[5,16,8,128]{3,2,1,0:T(8,128)} %all-reduce.6.cloned.1.call-done) | copy-start | bytes 983044
  346.2 128.1 %copy-start.1 = (f32[5,16,8,128]{3,2,1,0:T(8,128)S(1)}, f32[5,16,8,128]{3,2,1,0:T(8,128)}, u32[]{:S(2)}) copy-start(f32[5,16,8,128]{3,2,1,0:T(8,128)} %all-reduce.8.cloned.1.call-done) | copy-start | bytes 983044
  519.5 5.4 collective-permute-start.12
  523.5 8.9 %collective-permute-start.13 = (f32[2,16,4,128]{3,2,1,0:T(4,128)S(1)}, f32[2,16,4,128]{3,2,1,0:T(4,128)S(1)}, u32[]{:S(2)}, u32[]{:S(2)}) collective-permute-start(f32[2,16,4,128]{3,2,1,0:T(4,128)S(1)} %get-tuple-element.35), channel_id=1, source_target_pairs={{16,0},{32,16},{48,32},{17,1},{33,17},{49,33},{18,2},{34,18},{50,3... | collective-permute-start | bytes 196616 | tf_op jit(solution)/shard_map/ppermute | solution.py:20
  532.7 7.8 collective-permute-start.14
  537.2 14.8 %collective-permute-start.15 = (f32[2,16,16,4]{3,2,1,0:T(8,128)S(1)}, f32[2,16,16,4]{3,2,1,0:T(8,128)S(1)}, u32[]{:S(2)}, u32[]{:S(2)}) collective-permute-start(f32[2,16,16,4]{3,2,1,0:T(8,128)S(1)} %get-tuple-element.19), channel_id=1, source_target_pairs={{1,0},{2,1},{3,2},{4,3},{5,4},{6,5},{7,6},{8,7},{9,8},{10,9},{11,1... | collective-permute-start | bytes 24584 | tf_op jit(solution)/shard_map/ppermute | solution.py:20
  565.0 7.0 collective-permute-start.16
  570.7 12.9 %collective-permute-start.17 = (f32[2,16,4,128]{3,2,1,0:T(4,128)S(1)}, f32[2,16,4,128]{3,2,1,0:T(4,128)S(1)}, u32[]{:S(2)}, u32[]{:S(2)}) collective-permute-start(f32[2,16,4,128]{3,2,1,0:T(4,128)S(1)} %get-tuple-element.33), channel_id=1, source_target_pairs={{16,0},{32,16},{48,32},{17,1},{33,17},{49,33},{18,2},{34,18},{50,3... | collective-permute-start | bytes 196616 | tf_op jit(solution)/shard_map/ppermute | solution.py:20
  583.8 6.8 collective-permute-start.18
  585.1 12.2 %collective-permute-start.19 = (f32[2,16,16,4]{3,2,1,0:T(8,128)S(1)}, f32[2,16,16,4]{3,2,1,0:T(8,128)S(1)}, u32[]{:S(2)}, u32[]{:S(2)}) collective-permute-start(f32[2,16,16,4]{3,2,1,0:T(8,128)S(1)} %get-tuple-element.15), channel_id=1, source_target_pairs={{1,0},{2,1},{3,2},{4,3},{5,4},{6,5},{7,6},{8,7},{9,8},{10,9},{11,1... | collective-permute-start | bytes 24584 | tf_op jit(solution)/shard_map/ppermute | solution.py:20
  810.6 0.8 copy-start.6
Sparse Core Ops, SparseCore 0:
  62.3 73.9 all-reduce.5
  265.2 80.9 all-reduce.7
  610.7 71.6 all-reduce.9
where the time goes:
time: 821 us; the launch traced here: 819 us
  waiting for transfers between devices  332 us (40%)
  blocking collectives  212 us (26%)
  other arithmetic  115 us (14%)
  local copies, waits for them, and re-layouts  84.3 us (10%)
  starting transfers between devices  57.9 us (7%)
  between operations  18 us (2%)
    psum x2, blocking collectives, step_size(): lax.psum((grad_local, curv_local), ('mem', 'gy', 'gx'))  212 us
    psum x2, waiting for transfers between devices, per_device(): delta = lax.psum(delta_part, 'mem')  153 us
    ppermute x10, waiting for transfers between devices, extended(): after = lax.ppermute(initial, axis, down)  92.3 us
    psum x1, waiting for transfers between devices, per_device(): increment = lax.psum(partial_value, 'mem')  74.1 us
    ppermute x10, starting transfers between devices, extended(): before = lax.ppermute(last, axis, up)  44.7 us
    scatter-add x2, other arithmetic, per_device(): adjoint_part = jnp.zeros((increment.size,), jnp.float32).at[flat_cell].ad...  44 us
    gather x2, local copies, waits for them, and re-layouts, per_device(): misfit = jnp.where(inside, increment.reshape(-1)[flat_cell] - observed, 0.0)  42.6 us
    gather x2, local copies, waits for them, and re-layouts, per_device(): seen_step = delta.reshape(-1)[flat_cell]  39.1 us
  transfers between devices with their start and end apart: 23, of which 18 were waited for; matrix products, arithmetic and copies ran while one was open for 0% of the time, Pallas kernels for 0%

commit v1 on v0

v1 whole, which is shorter than its diff:
```python
import functools

import jax
import jax.numpy as jnp
import numpy as np
from jax import lax
from jax.experimental import pallas as pl
from jax.experimental.pallas import tpu as pltpu
from jax.sharding import PartitionSpec as P

MESH = pl.DeviceIdType.MESH
F32, BF16 = jnp.float32, jnp.bfloat16
MEM, GY, GX = 8, 4, 16
TILES = GY * GX
ITERS = 2
CHUNKS = 8
UP, OWN, DN = 0, 1, 2
LF, RT = 0, 1


def taps():
    offsets = np.arange(-4, 5).astype(np.float32)
    raw = np.exp(-offsets * offsets / np.float32(8.0))
    return (raw / raw.sum()).astype(np.float64)


def one_axis(length):
    weights = taps()
    distance = np.arange(length)[None, :] - np.arange(length)[:, None]
    inside = np.abs(distance) <= 4
    once = np.where(inside, weights[np.clip(distance + 4, 0, 8)], 0.0)
    return once, once @ once


def window(full, first_in, rows, first_out, cols):
    out = np.zeros((rows, cols))
    for i in range(rows):
        if 0 <= first_in + i < full.shape[0]:
            out[i] = full[first_in + i, first_out : first_out + cols]
    return out


def row_matrices():
    once, twice = one_axis(GY * 8)
    eye16, eye32 = np.eye(16), np.eye(32)
    ky = np.zeros((GY, 384, 256))
    kv = np.zeros((GY, 512, 256))
    for g in range(GY):
        for t in range(3):
            first = 8 * (g + t - 1)
            ky[g, t * 128 : t * 128 + 128, :128] = np.kron(eye16, window(once, first, 8, 8 * g, 8))
            ky[g, t * 128 : t * 128 + 128, 128:] = np.kron(eye16, window(twice, first, 8, 8 * g, 8))
        kv[g, :256] = np.kron(eye32, window(once, 8 * g, 8, 8 * g, 8))
        kv[g, 256:384] = np.kron(eye32, window(once, 8 * g - 4, 4, 8 * g, 8))
        kv[g, 384:] = np.kron(eye32, window(once, 8 * g + 8, 4, 8 * g, 8))
    return ky.astype(np.float32), kv.astype(np.float32)


def column_matrices():
    length = 128 * 3
    weights = one_axis(length)
    kx = np.zeros((3, 256, 256))
    for place, first in enumerate((0, 128, 256)):
        for k in range(2):
            rows = slice(k * 128, k * 128 + 128)
            kx[place, rows, :128] = window(weights[k], first, 128, first, 128).T
            kx[place, rows, 128:136] = window(weights[k], first - 8, 8, first, 128).T
            kx[place, rows, 136:144] = window(weights[k], first + 128, 8, first, 128).T
    return kx.astype(np.float32)


def row_selection():
    top = np.kron(np.eye(32), np.eye(8)[:, :4])
    bottom = np.kron(np.eye(32), np.eye(8)[:, 4:])
    return np.concatenate([top, bottom], axis=1).astype(np.float32)


def mm(a, b):
    return jnp.dot(a, b, preferred_element_type=F32, precision=lax.Precision.HIGHEST)


def halves(x):
    hi = x.astype(BF16)
    return hi, (x - hi.astype(F32)).astype(BF16)


def build_onehot(cell, onehot, t):
    index = lax.broadcasted_iota(jnp.int32, (512, 128), 0)

    def body(c, carry):
        for k in range(4):
            row = cell[t, pl.ds(c * 4 + k, 1), :]
            key = ((row & 127) >> 5) * 128 + ((row >> 7) & 127)
            onehot[t, c, :, k * 128 : k * 128 + 128] = jnp.where(index == key, 1.0, 0.0).astype(BF16)
        return carry

    lax.fori_loop(0, CHUNKS, body, 0)


def pert_at_obs(pert, table, cell, onehot, po):
    for v in range(5):
        for m in range(2):
            block = pert[(m * 5 + v) * 128 : (m * 5 + v + 1) * 128, :].astype(F32).T.astype(BF16)
            for xq in range(4):
                table[(v * 2 + m) * 32 : (v * 2 + m + 1) * 32, xq * 128 : xq * 128 + 128] = block[xq * 32 : xq * 32 + 32]
    index = lax.broadcasted_iota(jnp.int32, (32, 128), 0)

    def body(c, carry):
        got = jnp.dot(table[...], onehot[OWN, c], preferred_element_type=F32)
        for k in range(4):
            row = cell[OWN, pl.ds(c * 4 + k, 1), :]
            key = (row >> 14) * 32 + (row & 31)
            lanes = slice(k * 128, k * 128 + 128)
            for m in range(2):
                acc = jnp.zeros((32, 128), F32)
                for v in range(5):
                    acc = jnp.where(index + 32 * v == key, got[(v * 2 + m) * 32 : (v * 2 + m + 1) * 32, lanes], acc)
                po[OWN, m, pl.ds(c * 4 + k, 1), :] = jnp.sum(acc, axis=0, keepdims=True)
        return carry

    lax.fori_loop(0, CHUNKS, body, 0)


def observe(field, left, cell, onehot, po, out):
    for m in range(2):
        for xq in range(4):
            hi, lo = halves(field[xq * 32 : xq * 32 + 32, m * 128 : m * 128 + 128])
            left[m * 64 : m * 64 + 32, xq * 128 : xq * 128 + 128] = hi
            left[m * 64 + 32 : m * 64 + 64, xq * 128 : xq * 128 + 128] = lo
    index = lax.broadcasted_iota(jnp.int32, (32, 128), 0)

    def body(c, carry):
        got = jnp.dot(left[...], onehot[OWN, c], preferred_element_type=F32)
        for k in range(4):
            r = pl.ds(c * 4 + k, 1)
            lanes = slice(k * 128, k * 128 + 128)
            total = po[OWN, 0, r, :] * (got[0:32, lanes] + got[32:64, lanes])
            total += po[OWN, 1, r, :] * (got[64:96, lanes] + got[96:128, lanes])
            total = jnp.where(index == (cell[OWN, r, :] & 31), total, 0.0)
            out[r, :] = jnp.sum(total, axis=0, keepdims=True)
        return carry

    lax.fori_loop(0, CHUNKS, body, 0)


def spread(t, q, cell, onehot, po, acc, w):
    index = lax.broadcasted_iota(jnp.int32, (32, 128), 0)
    acc[...] = jnp.zeros_like(acc)

    def body(c, carry):
        columns = []
        for k in range(4):
            r = pl.ds(c * 4 + k, 1)
            mine = index == (cell[t, r, :] & 31)
            parts = []
            for m in range(2):
                value = po[t, m, r, :] * q[r, :]
                hi = value.astype(BF16).astype(F32)
                parts.append(jnp.where(mine, hi, 0.0))
                parts.append(jnp.where(mine, value - hi, 0.0))
            columns.append(jnp.concatenate(parts, axis=0).astype(BF16))
        acc[...] += lax.dot_general(
            jnp.concatenate(columns, axis=1), onehot[t, c], (((1,), (1,)), ((), ())), preferred_element_type=F32
        )
        return carry

    lax.fori_loop(0, CHUNKS, body, 0)
    for m in range(2):
        for xq in range(4):
            lanes = slice(xq * 128, xq * 128 + 128)
            w[t, m, xq * 32 : xq * 32 + 32, :] = acc[m * 64 : m * 64 + 32, lanes] + acc[m * 64 + 32 : m * 64 + 64, lanes]


def member_part(field, pert, out):
    turned = [field[:, m * 128 : m * 128 + 128].T for m in range(2)]
    for v in range(5):
        block = sum(pert[(m * 5 + v) * 128 : (m * 5 + v + 1) * 128, :].astype(F32) * turned[m] for m in range(2))
        for j in range(MEM):
            out[j, v] = block[j * 16 : j * 16 + 16]


def kernel(
    pert_in, ctrl_in, cell_in, flag_in, innov_in, prec_in, ky_in, kv_in, kx_in, sel_in,
    inc_out, change_out,
    pert, ctrl, cell, flag, innov, prec, ky, kv, kx, sel,
    onehot, table, left, acc, po, q, w,
    v_pack, v_edge, v_rows, v_strip, h_send, h_recv, w_send, w_recv, g_send, g_recv, r_send, r_recv,
    local_sem, send_sem, recv_sem,
):
    me_m, me_y, me_x = lax.axis_index("mem"), lax.axis_index("gy"), lax.axis_index("gx")
    up, dn = {"gy": lax.rem(me_y + 3, GY)}, {"gy": lax.rem(me_y + 1, GY)}
    lf, rt = {"gx": lax.rem(me_x + 15, GX)}, {"gx": lax.rem(me_x + 1, GX)}

    def member_peer(i):
        return {"mem": lax.rem(me_m + i, MEM)}

    def tile_peer(i):
        return {
            "gy": lax.rem(me_y + lax.rem(i // GX + 1, GY), GY),
            "gx": lax.rem(me_x + lax.rem(lax.rem(i, GX) + 1, GX), GX),
        }

    place = jnp.where(me_x == 0, 0, jnp.where(me_x == GX - 1, 2, 1))
    loads = [
        (ctrl_in, ctrl),
        (sel_in, sel),
        (cell_in, cell.at[OWN]),
        (pert_in, pert),
        (kv_in.at[me_y], kv),
        (kx_in.at[place], kx),
        (flag_in, flag),
        (innov_in, innov),
        (prec_in, prec),
        (ky_in.at[me_y], ky),
    ]
    loads = [pltpu.make_async_copy(src, dst, local_sem.at[i]) for i, (src, dst) in enumerate(loads)]
    for load in loads:
        load.start()

    barrier = pltpu.get_barrier_semaphore()
    for i in range(1, MEM):
        pl.semaphore_signal(barrier, inc=1, device_id=member_peer(i), device_id_type=MESH)

    def greet(i, carry):
        pl.semaphore_signal(barrier, inc=1, device_id=tile_peer(i), device_id_type=MESH)
        return carry

    lax.fori_loop(0, TILES - 1, greet, 0)

    sent = []
    used = [0]

    def copy(src, dst, device):
        i = used[0]
        used[0] += 1
        out = pltpu.make_async_remote_copy(
            src_ref=src, dst_ref=dst, send_sem=send_sem.at[i], recv_sem=recv_sem.at[i], device_id=device, device_id_type=MESH
        )
        out.start()
        sent.append(out)
        return out

    loads[0].wait()
    field = jnp.concatenate([ctrl[0:128, :].T, ctrl[128:256, :].T], axis=1)
    loads[1].wait()
    packed = mm(field, sel[...])
    v_pack[0], v_pack[1] = packed[:, :128], packed[:, 128:]
    for m in range(2):
        v_edge[0, m] = field[0:8, m * 128 : m * 128 + 128]
        v_edge[1, m] = field[120:128, m * 128 : m * 128 + 128]
    loads[2].wait()

    pl.semaphore_wait(barrier, MEM - 1 + TILES - 1)

    first, last = pl.ds(0, 8), pl.ds(120, 8)
    halo = [
        copy(v_pack.at[0], v_rows.at[1], up),
        copy(v_pack.at[1], v_rows.at[0], dn),
        copy(v_edge.at[0], v_strip.at[RT, pl.ds(0, 2)], lf),
        copy(v_edge.at[1], v_strip.at[LF, pl.ds(0, 2)], rt),
        copy(v_pack.at[0, first], v_strip.at[RT, 3], {**up, **lf}),
        copy(v_pack.at[0, last], v_strip.at[LF, 3], {**up, **rt}),
        copy(v_pack.at[1, first], v_strip.at[RT, 2], {**dn, **lf}),
        copy(v_pack.at[1, last], v_strip.at[LF, 2], {**dn, **rt}),
    ]
    cells = [copy(cell.at[OWN], cell.at[DN], up), copy(cell.at[OWN], cell.at[UP], dn)]

    build_onehot(cell, onehot, OWN)
    loads[3].wait()
    pert_at_obs(pert, table, cell, onehot, po)
    perts = [copy(po.at[OWN], po.at[DN], up), copy(po.at[OWN], po.at[UP], dn)]

    for load in loads[4:]:
        load.wait()
    rows_v = mm(field, kv[0:256])
    for one in halo:
        one.wait_recv()
    rows_v += mm(jnp.concatenate([v_rows[0], v_rows[1]], axis=1), kv[256:512])
    strips = [jnp.concatenate([v_strip[side, i] for i in range(4)], axis=1) for side in (LF, RT)]
    strips = mm(jnp.concatenate(strips, axis=0), kv[...])
    smoothed = mm(kx[0:128, 0:128], rows_v) + mm(kx[0:128, 128:144], strips)

    def sum_members(phase):
        base = used[0]
        used[0] += 1
        for i in range(1, MEM):
            pltpu.make_async_remote_copy(
                src_ref=h_send.at[phase],
                dst_ref=h_recv.at[phase, i - 1],
                send_sem=send_sem.at[base],
                recv_sem=recv_sem.at[base],
                device_id=member_peer(i),
                device_id_type=MESH,
            ).start()
        every = pltpu.make_async_copy(h_recv.at[phase], h_recv.at[phase], recv_sem.at[base])
        sent_all.append((h_recv.at[phase], base))

        def total():
            every.wait()
            out = h_send[phase]
            for i in range(MEM - 1):
                out += h_recv[phase, i]
            return out

        return total

    sent_all = []

    def share_levels(k):
        base = used[0]
        used[0] += 1
        for i in range(1, MEM):
            pltpu.make_async_remote_copy(
                src_ref=r_send.at[k, lax.rem(me_m + i, MEM)],
                dst_ref=r_recv.at[k, i - 1],
                send_sem=send_sem.at[base],
                recv_sem=recv_sem.at[base],
                device_id=member_peer(i),
                device_id_type=MESH,
            ).start()
        sent_all.append((r_recv.at[k], base))
        every = pltpu.make_async_copy(r_recv.at[k], r_recv.at[k], recv_sem.at[base])

        def total():
            every.wait()
            out = r_send[k, me_m]
            for i in range(MEM - 1):
                out += r_recv[k, i]
            return out

        return total

    observe(smoothed, left, cell, onehot, po, h_send.at[0])
    h_send[0, 32:40, :] = jnp.zeros((8, 128), F32)
    total = sum_members(0)
    for one in cells:
        one.wait_recv()
    build_onehot(cell, onehot, UP)
    build_onehot(cell, onehot, DN)
    state = field
    seen = total()[0:32]
    lane = lax.broadcasted_iota(jnp.int32, (1, 128), 1)
    levels = []
    changes = jnp.zeros_like(field)
    for it in range(ITERS):
        misfit = seen - innov[...]
        weight = jnp.where(flag[...] == 1, 1.0 / jnp.sqrt(1.0 + misfit * misfit), 1.0)
        inverse = prec[...] * weight
        q[it, OWN] = inverse * misfit
        rows = [copy(q.at[it, OWN], q.at[it, DN], up), copy(q.at[it, OWN], q.at[it, UP], dn)]
        spread(OWN, q.at[it, OWN], cell, onehot, po, acc, w)
        if it == 0:
            for one in perts:
                one.wait_recv()
        else:
            member_part(smoothed, pert, r_send.at[0])
            levels.append(share_levels(0))
        rows[1].wait_recv()
        spread(UP, q.at[it, UP], cell, onehot, po, acc, w)
        rows[0].wait_recv()
        spread(DN, q.at[it, DN], cell, onehot, po, acc, w)
        for t in range(3):
            for m in range(2):
                w_send[it, 0, t, m] = w[t, m, 0:8, :]
                w_send[it, 1, t, m] = w[t, m, 120:128, :]
        sides = [copy(w_send.at[it, 0], w_recv.at[it, RT], lf), copy(w_send.at[it, 1], w_recv.at[it, LF], rt)]
        along = sum(
            mm(jnp.concatenate([w[t, 0], w[t, 1]], axis=0), ky[t * 128 : t * 128 + 128, :]) for t in range(3)
        )
        once = mm(kx[0:128, 0:128], jnp.concatenate([along[0:128, 0:128], along[128:256, 0:128]], axis=1))
        twice = mm(kx[128:256, 0:128], jnp.concatenate([along[0:128, 128:256], along[128:256, 128:256]], axis=1))
        for one in sides:
            one.wait_recv()
        edge = sum(
            mm(
                jnp.concatenate([w_recv[it, side, t, m] for m in range(2) for side in (LF, RT)], axis=0),
                ky[t * 128 : t * 128 + 128, :],
            )
            for t in range(3)
        )
        once += mm(kx[0:128, 128:144], jnp.concatenate([edge[0:16, 0:128], edge[16:32, 0:128]], axis=1))
        twice += mm(kx[128:256, 128:144], jnp.concatenate([edge[0:16, 128:256], edge[16:32, 128:256]], axis=1))
        grad = state + once
        change = smoothed + twice
        observe(change, left, cell, onehot, po, h_send.at[it + 1])
        norm = jnp.sum((grad * grad).reshape(16, 8, 256), axis=0)
        h_send[it + 1, 32:40, :] = norm[:, 0:128] + norm[:, 128:256]
        total = sum_members(it + 1)
        if it == ITERS - 1:
            member_part(change, pert, r_send.at[1])
            levels.append(share_levels(1))
        totals = total()
        delta = totals[0:32]
        norm = jnp.sum(totals[32:40], axis=0, keepdims=True)
        curv = jnp.sum(inverse * delta * delta, axis=0, keepdims=True)
        norm = norm + pltpu.roll(norm, 64, 1)
        curv = curv + pltpu.roll(curv, 64, 1)
        both = jnp.where(lane < 64, norm, curv)
        g_send[it] = both
        base = used[0]
        used[0] += 1

        def scatter_scalars(i, carry):
            pltpu.make_async_remote_copy(
                src_ref=g_send.at[it],
                dst_ref=g_recv.at[it, i],
                send_sem=send_sem.at[base],
                recv_sem=recv_sem.at[base],
                device_id=tile_peer(i),
                device_id_type=MESH,
            ).start()
            return carry

        lax.fori_loop(0, TILES - 1, scatter_scalars, 0)
        sent_all.append((g_recv.at[it], base))
        pltpu.make_async_copy(g_recv.at[it], g_recv.at[it], recv_sem.at[base]).wait()
        both = both + jnp.sum(g_recv[it], axis=0)
        norm = jnp.sum(jnp.where(lane < 64, both, 0.0), axis=1, keepdims=True)
        curv = jnp.sum(jnp.where(lane < 64, 0.0, both), axis=1, keepdims=True)
        step = norm / (norm + curv)
        state = state - step * grad
        changes = changes + step * grad
        if it < ITERS - 1:
            smoothed = smoothed - step * change
            seen = seen - step * delta
    inc_out[...] = levels[0]() - step.reshape(1, 1, 1) * levels[1]()
    for m in range(2):
        change_out[m * 128 : m * 128 + 128, :] = changes[:, m * 128 : m * 128 + 128].T
    for one in sent:
        one.wait_send()
    for ref, i in sent_all:
        pltpu.make_async_copy(ref, ref, send_sem.at[i]).wait()


def per_device(perturbations, control, background, obs_cell, huber_flag, innovation, precision):
    ky, kv = row_matrices()
    kx, sel = column_matrices(), row_selection()
    args = (
        perturbations.reshape(1280, 128), control.reshape(256, 128), obs_cell, huber_flag, innovation, precision,
        jnp.asarray(ky), jnp.asarray(kv), jnp.asarray(kx), jnp.asarray(sel),
    )
    i32 = jnp.int32
    inc, change = pl.pallas_call(
        kernel,
        out_shape=(jax.ShapeDtypeStruct((5, 16, 128), F32), jax.ShapeDtypeStruct((256, 128), F32)),
        in_specs=[pl.BlockSpec(memory_space=pltpu.HBM)] * len(args),
        out_specs=(pl.BlockSpec(memory_space=pltpu.VMEM),) * 2,
        scratch_shapes=[
            pltpu.VMEM((1280, 128), BF16),
            pltpu.VMEM((256, 128), F32),
            pltpu.VMEM((3, 32, 128), i32),
            pltpu.VMEM((32, 128), i32),
            pltpu.VMEM((32, 128), F32),
            pltpu.VMEM((32, 128), F32),
            pltpu.VMEM((384, 256), F32),
            pltpu.VMEM((512, 256), F32),
            pltpu.VMEM((256, 256), F32),
            pltpu.VMEM((256, 256), F32),
            pltpu.VMEM((3, CHUNKS, 512, 512), BF16),
            pltpu.VMEM((320, 512), BF16),
            pltpu.VMEM((128, 512), BF16),
            pltpu.VMEM((128, 512), F32),
            pltpu.VMEM((3, 2, 32, 128), F32),
            pltpu.VMEM((ITERS, 3, 32, 128), F32),
            pltpu.VMEM((3, 2, 128, 128), F32),
            pltpu.VMEM((2, 128, 128), F32),
            pltpu.VMEM((2, 2, 8, 128), F32),
            pltpu.VMEM((2, 128, 128), F32),
            pltpu.VMEM((2, 4, 8, 128), F32),
            pltpu.VMEM((ITERS + 1, 40, 128), F32),
            pltpu.VMEM((ITERS + 1, MEM - 1, 40, 128), F32),
            pltpu.VMEM((ITERS, 2, 3, 2, 8, 128), F32),
            pltpu.VMEM((ITERS, 2, 3, 2, 8, 128), F32),
            pltpu.VMEM((ITERS, 1, 128), F32),
            pltpu.VMEM((ITERS, TILES - 1, 1, 128), F32),
            pltpu.VMEM((2, MEM, 5, 16, 128), F32),
            pltpu.VMEM((2, MEM - 1, 5, 16, 128), F32),
            pltpu.SemaphoreType.DMA((10,)),
            pltpu.SemaphoreType.DMA((32,)),
            pltpu.SemaphoreType.DMA((32,)),
        ],
        compiler_params=pltpu.CompilerParams(collective_id=0, has_side_effects=True, vmem_limit_bytes=63 * 2**20 + 2**19),
    )(*args)
    return background + inc.reshape(background.shape), control - change.reshape(control.shape)


def solution(mesh):
    grid = P("mem", None, "gy", "gx")
    table = P("gy", "gx")
    return jax.shard_map(
        per_device,
        mesh=mesh,
        in_specs=(P("mem", None, None, "gy", "gx"), grid, P(None, "mem", "gy", "gx"), table, table, table, table),
        out_specs=(P(None, "mem", "gy", "gx"), grid),
        check_vma=False,
    )
```

time: 821 us -> 109 us (0.13)
  waiting for transfers between devices: 332 us -> 0 us
  blocking collectives: 212 us -> 0 us
  other arithmetic: 115 us -> 2.98 us
  Pallas kernels: 0 us -> 105 us
  local copies, waits for them, and re-layouts: 84.3 us -> 0.01 us
  starting transfers between devices: 57.9 us -> 0 us
  between operations: 18 us -> 0.66 us
    psum x3 -> x0, waiting for transfers between devices: 227 us -> none  [the longest x2 153 us: per_device(): delta = lax.psum(delta_part, 'mem')]
    psum x2 -> x0, blocking collectives: 212 us -> none  [step_size(): lax.psum((grad_local, curv_local), ('mem', 'gy', 'gx'))]
    ppermute x20 -> x0, waiting for transfers between devices: 105 us -> none  [the longest x10 92.3 us: extended(): after = lax.ppermute(initial, axis, down)]
    pallas_call x0 -> x1, Pallas kernels: none -> 105 us  [per_device(): pl.pallas_call(kernel, out_shape=(jax.ShapeDtypeStruct((5, 16, 128), F32)...]
    gather x4 -> x0, local copies, waits for them, and re-layouts: 81.7 us -> none  [the longest x2 42.6 us: per_device(): misfit = jnp.where(inside, increment.reshape(-1)[flat_cell] - observed, 0.0)]
    ppermute x20 -> x0, starting transfers between devices: 57.8 us -> none  [the longest x10 44.7 us: extended(): before = lax.ppermute(last, axis, up)]
    add x9 -> x1, other arithmetic: 50.2 us -> 1.4 us  [per_device(): background + inc.reshape(background.shape)]
    scatter-add x2 -> x0, other arithmetic: 44 us -> none  [per_device(): adjoint_part = jnp.zeros((increment.size,), jnp.float32).at[flat_cell].ad...]
  transfers between devices with their start and end apart: 23 -> 0, of which waited for: 18 -> 0; matrix products, arithmetic and copies ran while one was open for 0% -> 0% of each run, Pallas kernels for 0% -> 0%
where the time goes in v1:
time: 109 us
  Pallas kernels  105 us (96%)
  other arithmetic  2.98 us (3%)
    pallas_call x1, Pallas kernels, per_device(): pl.pallas_call(kernel, out_shape=(jax.ShapeDtypeStruct((5, 16, 128), F32)...  105 us

profile of v1, /device:TPU:1, one launch (start us, length us, event | category | flops | bytes accessed | tf_op | source)
XLA Modules:
  0.0 108.7 jit_solution(10697825446443905959)
XLA Ops:
  0.6 0.0 copy-start.1
  0.6 0.0 copy-start
  0.7 105.1 %shard_map.122 = (f32[5,16,128]{2,1,0:T(8,128)}, f32[256,128]{1,0:T(8,128)}) custom-call(bf16[1280,128]{1,0:T(8,128)(2,1)} %bitcast.6, f32[256,128]{1,0:T(8,128)} %bitcast.5, s32[32,128]{1,0:T(8,128)} %cell_in.1, s32[32,128]{1,0:T(8,128)} %flag_in.1, f32[32,128]{1,0:T(8,128)} %innov_in.1, f32[32,128]{1,0:T(8,128)} %prec_in.1, ...), custom_call_target="tpu_custom_call" | custom-call | tf_op jit(solution)/shard_map/pallas_call | solution.py:443
  105.7 0.0 copy-done.1
  105.7 1.4 %bitcast_add_fusion = f32[5,2,8,128]{3,2,1,0:T(8,128)} fusion(f32[5,2,8,128]{3,2,1,0:T(8,128)S(1)} %copy-done.1, f32[5,16,128]{2,1,0:T(8,128)} %get-tuple-element.4), kind=kLoop, calls=%fused_computation | loop fusion | flops 10240 | bytes 122880 | tf_op jit(solution)/shard_map/add | solution.py:484
  107.1 0.0 copy-done
  107.2 1.6 %sub.3 = f32[2,16,8,128]{3,2,1,0:T(8,128)} subtract(f32[2,16,8,128]{3,2,1,0:T(8,128)S(1)} %copy-done, f32[2,16,8,128]{3,2,1,0:T(8,128)} %bitcast.7) | non-fusion elementwise | flops 32768 | bytes 393216 | tf_op jit(solution)/shard_map/sub | solution.py:484
Async XLA Ops:
  0.6 105.1 %copy-start.1 = (f32[5,2,8,128]{3,2,1,0:T(8,128)S(1)}, f32[5,2,8,128]{3,2,1,0:T(8,128)}, u32[]{:S(2)}) copy-start(f32[5,2,8,128]{3,2,1,0:T(8,128)} %param.13) | copy-start | bytes 122884
  0.6 106.5 %copy-start = (f32[2,16,8,128]{3,2,1,0:T(8,128)S(1)}, f32[2,16,8,128]{3,2,1,0:T(8,128)}, u32[]{:S(2)}) copy-start(f32[2,16,8,128]{3,2,1,0:T(8,128)} %param.12) | copy-start | bytes 393220

commit v2 on v1

v2 whole, which is shorter than its diff:
```python
import functools

import jax
import jax.numpy as jnp
import numpy as np
from jax import lax
from jax.experimental import pallas as pl
from jax.experimental.pallas import tpu as pltpu
from jax.sharding import PartitionSpec as P

MESH = pl.DeviceIdType.MESH
F32, BF16 = jnp.float32, jnp.bfloat16
MEM, GY, GX = 8, 4, 16
TILES = GY * GX
ITERS = 2
UP, OWN, DN = 0, 1, 2
LF, RT = 0, 1


def taps():
    offsets = np.arange(-4, 5).astype(np.float32)
    raw = np.exp(-offsets * offsets / np.float32(8.0))
    return (raw / raw.sum()).astype(np.float64)


def one_axis(length):
    weights = taps()
    distance = np.arange(length)[None, :] - np.arange(length)[:, None]
    inside = np.abs(distance) <= 4
    once = np.where(inside, weights[np.clip(distance + 4, 0, 8)], 0.0)
    return once, once @ once


def window(full, first_in, rows, first_out, cols):
    out = np.zeros((rows, cols))
    for i in range(rows):
        if 0 <= first_in + i < full.shape[0]:
            out[i] = full[first_in + i, first_out : first_out + cols]
    return out


def row_matrices():
    once, twice = one_axis(GY * 8)
    eye16, eye32 = np.eye(16), np.eye(32)
    ky = np.zeros((GY, 384, 256))
    kv = np.zeros((GY, 512, 256))
    for g in range(GY):
        for t in range(3):
            first = 8 * (g + t - 1)
            ky[g, t * 128 : t * 128 + 128, :128] = np.kron(eye16, window(once, first, 8, 8 * g, 8))
            ky[g, t * 128 : t * 128 + 128, 128:] = np.kron(eye16, window(twice, first, 8, 8 * g, 8))
        kv[g, :256] = np.kron(eye32, window(once, 8 * g, 8, 8 * g, 8))
        kv[g, 256:384] = np.kron(eye32, window(once, 8 * g - 4, 4, 8 * g, 8))
        kv[g, 384:] = np.kron(eye32, window(once, 8 * g + 8, 4, 8 * g, 8))
    return ky.astype(np.float32), kv.astype(np.float32)


def column_matrices():
    length = 128 * 3
    weights = one_axis(length)
    kx = np.zeros((3, 256, 256))
    for place, first in enumerate((0, 128, 256)):
        for k in range(2):
            rows = slice(k * 128, k * 128 + 128)
            kx[place, rows, :128] = window(weights[k], first, 128, first, 128).T
            kx[place, rows, 128:136] = window(weights[k], first - 8, 8, first, 128).T
            kx[place, rows, 136:144] = window(weights[k], first + 128, 8, first, 128).T
    return kx.astype(np.float32)


def split(matrix):
    hi = matrix.astype(BF16)
    return hi, (matrix - hi.astype(np.float32)).astype(BF16)


def stack(matrix, axis):
    hi, lo = split(matrix)
    return np.concatenate([hi, hi, lo], axis=axis)


def row_selection():
    top = np.kron(np.eye(32), np.eye(8)[:, :4])
    bottom = np.kron(np.eye(32), np.eye(8)[:, 4:])
    return np.concatenate([top, bottom], axis=1).astype(np.float32)


def mm(a, b):
    return jnp.dot(a, b, preferred_element_type=F32, precision=lax.Precision.HIGHEST)


def halves(x):
    hi = x.astype(BF16)
    return hi, (x - hi.astype(F32)).astype(BF16)


def times_matrix(x, stacked):
    hi, lo = halves(x)
    return jnp.dot(jnp.concatenate([hi, lo, hi], axis=1), stacked, preferred_element_type=F32)


def matrix_times(stacked, x):
    hi, lo = halves(x)
    parts = [hi, lo, hi]
    more = stacked.shape[1] - 3 * x.shape[0]
    if more:
        parts.append(jnp.zeros((more, x.shape[1]), BF16))
    return jnp.dot(stacked, jnp.concatenate(parts, axis=0), preferred_element_type=F32)


def table_rows(body):
    def four(c, carry):
        for k in range(4):
            body(pl.ds(c * 4 + k, 1), pl.ds(pl.multiple_of(c * 512 + k * 128, 128), 128))
        return carry

    lax.fori_loop(0, 8, four, 0)


def build_onehot(cell, onehot, t):
    index = lax.broadcasted_iota(jnp.int32, (256, 128), 0)

    def body(r, lanes):
        row = cell[t, r, :]
        key = ((row & 127) >> 6) * 128 + ((row >> 7) & 127)
        onehot[t, :, lanes] = jnp.where(index == key, 1.0, 0.0).astype(BF16)

    table_rows(body)


def pert_at_obs(pert, table, cell, onehot, got, po):
    for v in range(5):
        for m in range(2):
            block = pert[(m * 5 + v) * 128 : (m * 5 + v + 1) * 128, :].astype(F32).T.astype(BF16)
            for xq in range(2):
                table[(v * 2 + m) * 64 : (v * 2 + m + 1) * 64, xq * 128 : xq * 128 + 128] = block[xq * 64 : xq * 64 + 64]
    index = lax.broadcasted_iota(jnp.int32, (64, 128), 0)
    got[...] = jnp.dot(table[...], onehot[OWN], preferred_element_type=F32)

    def body(r, lanes):
        row = cell[OWN, r, :]
        key = (row >> 14) * 64 + (row & 63)
        for m in range(2):
            acc = jnp.zeros((64, 128), F32)
            for v in range(5):
                acc = jnp.where(index + 64 * v == key, got[(v * 2 + m) * 64 : (v * 2 + m + 1) * 64, lanes], acc)
            po[OWN, m, r, :] = jnp.sum(acc, axis=0, keepdims=True)

    table_rows(body)


def observe(field, left, cell, onehot, got, po, out):
    for m in range(2):
        for xq in range(2):
            hi, lo = halves(field[xq * 64 : xq * 64 + 64, m * 128 : m * 128 + 128])
            left[m * 128 : m * 128 + 64, xq * 128 : xq * 128 + 128] = hi
            left[m * 128 + 64 : m * 128 + 128, xq * 128 : xq * 128 + 128] = lo
    index = lax.broadcasted_iota(jnp.int32, (64, 128), 0)
    got[0:256, :] = jnp.dot(left[...], onehot[OWN], preferred_element_type=F32)

    def body(r, lanes):
        total = po[OWN, 0, r, :] * (got[0:64, lanes] + got[64:128, lanes])
        total += po[OWN, 1, r, :] * (got[128:192, lanes] + got[192:256, lanes])
        total = jnp.where(index == (cell[OWN, r, :] & 63), total, 0.0)
        out[r, :] = jnp.sum(total, axis=0, keepdims=True)

    table_rows(body)


def spread(t, q, cell, onehot, po, values, w):
    index = lax.broadcasted_iota(jnp.int32, (64, 128), 0)

    def body(r, lanes):
        mine = index == (cell[t, r, :] & 63)
        for m in range(2):
            value = po[t, m, r, :] * q[r, :]
            hi = value.astype(BF16).astype(F32)
            values[m * 128 : m * 128 + 64, lanes] = jnp.where(mine, hi, 0.0).astype(BF16)
            values[m * 128 + 64 : m * 128 + 128, lanes] = jnp.where(mine, value - hi, 0.0).astype(BF16)

    table_rows(body)
    got = lax.dot_general(values[...], onehot[t], (((1,), (1,)), ((), ())), preferred_element_type=F32)
    for m in range(2):
        for xq in range(2):
            lanes = slice(xq * 128, xq * 128 + 128)
            w[m * 128 + xq * 64 : m * 128 + xq * 64 + 64, t * 128 : t * 128 + 128] = (
                got[m * 128 : m * 128 + 64, lanes] + got[m * 128 + 64 : m * 128 + 128, lanes]
            )


def member_part(field, pert, out):
    turned = [field[:, m * 128 : m * 128 + 128].T for m in range(2)]
    for v in range(5):
        block = sum(pert[(m * 5 + v) * 128 : (m * 5 + v + 1) * 128, :].astype(F32) * turned[m] for m in range(2))
        for j in range(MEM):
            out[j, v] = block[j * 16 : j * 16 + 16]


def kernel(
    pert_in, ctrl_in, back_in, cell_in, flag_in, innov_in, prec_in, ky_in, kvo_in, kvh_in, kxo_in, kxs_in, sel_in,
    inc_out, state_out,
    pert, ctrl, back, cell, flag, innov, prec, ky, kvo, kvh, kxo, kxs, sel,
    onehot, table, left, values, got, po, q, w, exch, part, edges, fields,
    v_pack, v_edge, v_rows, v_strip, h_send, h_recv, w_send, w_recv, g_send, g_recv, r_send, r_recv,
    local_sem, send_sem, recv_sem, far_sem,
):
    me_m, me_y, me_x = lax.axis_index("mem"), lax.axis_index("gy"), lax.axis_index("gx")
    up, dn = {"gy": lax.rem(me_y + 3, GY)}, {"gy": lax.rem(me_y + 1, GY)}
    lf, rt = {"gx": lax.rem(me_x + 15, GX)}, {"gx": lax.rem(me_x + 1, GX)}

    def member_peer(i):
        return {"mem": lax.rem(me_m + i, MEM)}

    def tile_peer(i):
        return {
            "gy": lax.rem(me_y + lax.rem(i // GX + 1, GY), GY),
            "gx": lax.rem(me_x + lax.rem(lax.rem(i, GX) + 1, GX), GX),
        }

    place = jnp.where(me_x == 0, 0, jnp.where(me_x == GX - 1, 2, 1))
    loads = [
        (ctrl_in, ctrl),
        (sel_in, sel),
        (cell_in, cell.at[OWN]),
        (pert_in, pert),
        (kvo_in.at[me_y], kvo),
        (kvh_in.at[me_y], kvh),
        (kxo_in.at[place], kxo),
        (kxs_in.at[place], kxs),
        (flag_in, flag.at[OWN]),
        (innov_in, innov.at[OWN]),
        (prec_in, prec.at[OWN]),
        (ky_in.at[me_y], ky),
        (back_in, back),
    ]
    loads = [pltpu.make_async_copy(src, dst, local_sem.at[i]) for i, (src, dst) in enumerate(loads)]
    for load in loads:
        load.start()

    barrier = pltpu.get_barrier_semaphore()
    for device in (up, dn, lf, rt, {**up, **lf}, {**up, **rt}, {**dn, **lf}, {**dn, **rt}):
        pl.semaphore_signal(barrier, inc=1, device_id=device, device_id_type=MESH)
    for i in range(1, MEM):
        pl.semaphore_signal(barrier, inc=1, device_id=member_peer(i), device_id_type=MESH)

    sent, sent_all = [], []
    used = [0]

    def copy(src, dst, device):
        i = used[0]
        used[0] += 1
        out = pltpu.make_async_remote_copy(
            src_ref=src, dst_ref=dst, send_sem=send_sem.at[i], recv_sem=recv_sem.at[i], device_id=device, device_id_type=MESH
        )
        out.start()
        sent.append(out)
        return out

    def up_and_dn(ref):
        return [copy(ref.at[OWN], ref.at[DN], up), copy(ref.at[OWN], ref.at[UP], dn)]

    def to_members(source, into):
        base = used[0]
        used[0] += 1
        for i in range(1, MEM):
            pltpu.make_async_remote_copy(
                src_ref=source(i),
                dst_ref=into.at[i - 1],
                send_sem=send_sem.at[base],
                recv_sem=recv_sem.at[base],
                device_id=member_peer(i),
                device_id_type=MESH,
            ).start()
        sent_all.append((into, base))
        return pltpu.make_async_copy(into, into, recv_sem.at[base])

    loads[0].wait()
    field = jnp.concatenate([ctrl[0:128, :].T, ctrl[128:256, :].T], axis=1)
    loads[1].wait()
    packed = mm(field, sel[...])
    v_pack[0], v_pack[1] = packed[:, :128], packed[:, 128:]
    for m in range(2):
        v_edge[0, m] = field[0:8, m * 128 : m * 128 + 128]
        v_edge[1, m] = field[120:128, m * 128 : m * 128 + 128]
    loads[2].wait()

    pl.semaphore_wait(barrier, 8 + MEM - 1)

    first, last = pl.ds(0, 8), pl.ds(120, 8)
    halo = [
        copy(v_pack.at[0], v_rows.at[1], up),
        copy(v_pack.at[1], v_rows.at[0], dn),
        copy(v_pack.at[0, first], v_strip.at[RT, 3], {**up, **lf}),
        copy(v_pack.at[0, last], v_strip.at[LF, 3], {**up, **rt}),
        copy(v_pack.at[1, first], v_strip.at[RT, 2], {**dn, **lf}),
        copy(v_pack.at[1, last], v_strip.at[LF, 2], {**dn, **rt}),
        copy(v_edge.at[0], v_strip.at[RT, pl.ds(0, 2)], lf),
        copy(v_edge.at[1], v_strip.at[LF, pl.ds(0, 2)], rt),
    ]
    tables = up_and_dn(cell)

    build_onehot(cell, onehot, OWN)
    loads[3].wait()
    pert_at_obs(pert, table, cell, onehot, got, po)
    tables += up_and_dn(po)

    for load in loads[4:]:
        load.wait()
    rows_v = times_matrix(field, kvo[...])
    for one in halo:
        one.wait_recv()
    for offset in (2, GX - 2):
        pl.semaphore_signal(far_sem.at[0], inc=1, device_id={"gx": lax.rem(me_x + offset, GX)}, device_id_type=MESH)
    for ref in (innov, prec, flag):
        tables += up_and_dn(ref)
    rows_v += times_matrix(jnp.concatenate([v_rows[0], v_rows[1]], axis=1), kvh[...])
    near = [jnp.concatenate([v_strip[side, 0], v_strip[side, 1]], axis=1) for side in (LF, RT)]
    far = [jnp.concatenate([v_strip[side, 2], v_strip[side, 3]], axis=1) for side in (LF, RT)]
    strips = times_matrix(jnp.concatenate(near, axis=0), kvo[...]) + times_matrix(jnp.concatenate(far, axis=0), kvh[...])
    smoothed = matrix_times(kxo[0:128, :], rows_v) + matrix_times(kxs[0:128, :], strips)

    def members_total(phase):
        out = h_send[phase]
        for i in range(MEM - 1):
            out += h_recv[phase, i]
        return out

    def levels_total(k):
        out = r_send[k, me_m]
        for i in range(MEM - 1):
            out += r_recv[k, i]
        return out

    observe(smoothed, left, cell, onehot, got, po, h_send.at[0])
    h_send[0, 32:40, :] = jnp.zeros((8, 128), F32)
    arrived = to_members(lambda i: h_send.at[0], h_recv.at[0])
    for one in tables[0:2]:
        one.wait_recv()
    build_onehot(cell, onehot, UP)
    build_onehot(cell, onehot, DN)
    arrived.wait()
    exch[0, OWN] = members_total(0)[0:32]
    around = up_and_dn(exch.at[0])
    pl.semaphore_wait(far_sem.at[0], 2)
    for offset in (4, GX - 4):
        pl.semaphore_signal(far_sem.at[1], inc=1, device_id={"gx": lax.rem(me_x + offset, GX)}, device_id_type=MESH)
    state = field
    lane = lax.broadcasted_iota(jnp.int32, (1, 128), 1)
    levels = []

    def terms(t, seen):
        misfit = seen - innov[t]
        weight = jnp.where(flag[t] == 1, 1.0 / jnp.sqrt(1.0 + misfit * misfit), 1.0)
        inverse = prec[t] * weight
        q[t] = inverse * misfit
        return inverse

    def x_stage(along, rows):
        return [
            jnp.concatenate([along[0:rows, k * 128 : k * 128 + 128], along[rows : 2 * rows, k * 128 : k * 128 + 128]], axis=1)
            for k in range(2)
        ]

    for it in range(ITERS):
        for t in (OWN, UP, DN):
            if it == 0:
                if t == UP:
                    for one in tables[2:]:
                        one.wait_recv()
                    around[1].wait_recv()
                elif t == DN:
                    around[0].wait_recv()
                seen = exch[0, t]
            else:
                seen = exch[0, t] - step * exch[1, t]
            inverse_t = terms(t, seen)
            if t == OWN:
                inverse = inverse_t
            spread(t, q.at[t], cell, onehot, po, values, w)
        for m in range(2):
            w_send[it, 0, m * 8 : m * 8 + 8, :] = w[m * 128 : m * 128 + 8, :]
            w_send[it, 1, m * 8 : m * 8 + 8, :] = w[m * 128 + 120 : m * 128 + 128, :]
        sides = [copy(w_send.at[it, 0], w_recv.at[it, RT], lf), copy(w_send.at[it, 1], w_recv.at[it, LF], rt)]
        if it == ITERS - 1:
            member_part(smoothed, pert, r_send.at[0])
            levels.append(to_members(lambda i: r_send.at[0, lax.rem(me_m + i, MEM)], r_recv.at[0]))
        once, twice = x_stage(times_matrix(w[...], ky[...]), 128)
        part[0] = matrix_times(kxo[0:128, :], once)
        part[1] = matrix_times(kxo[128:256, :], twice)
        for one in sides:
            one.wait_recv()
        edge = [w_recv[it, side, m * 8 : m * 8 + 8, :] for m in range(2) for side in (LF, RT)]
        edges[...] = times_matrix(jnp.concatenate(edge, axis=0), ky[...])
        edge_once, edge_twice = x_stage(edges, 16)
        fields[it, 0] = matrix_times(kxs[0:128, :], edge_once)
        fields[it, 1] = matrix_times(kxs[128:256, :], edge_twice)
        grad = state + (part[0] + fields[it, 0])
        change = smoothed + (part[1] + fields[it, 1])
        observe(change, left, cell, onehot, got, po, h_send.at[it + 1])
        norm = jnp.sum((grad * grad).reshape(16, 8, 256), axis=0)
        h_send[it + 1, 32:40, :] = norm[:, 0:128] + norm[:, 128:256]
        arrived = to_members(lambda i: h_send.at[it + 1], h_recv.at[it + 1])
        if it == ITERS - 1:
            member_part(change, pert, r_send.at[1])
            levels.append(to_members(lambda i: r_send.at[1, lax.rem(me_m + i, MEM)], r_recv.at[1]))
        arrived.wait()
        totals = members_total(it + 1)
        delta = totals[0:32]
        norm = jnp.sum(totals[32:40], axis=0, keepdims=True)
        curv = jnp.sum(inverse * delta * delta, axis=0, keepdims=True)
        norm = norm + pltpu.roll(norm, 64, 1)
        curv = curv + pltpu.roll(curv, 64, 1)
        both = jnp.where(lane < 64, norm, curv)
        g_send[it] = both
        if it == 0:
            pl.semaphore_wait(far_sem.at[1], 2)
        base = used[0]
        used[0] += 1

        def to_tiles(i, carry):
            pltpu.make_async_remote_copy(
                src_ref=g_send.at[it],
                dst_ref=g_recv.at[it, i],
                send_sem=send_sem.at[base],
                recv_sem=recv_sem.at[base],
                device_id=tile_peer(i),
                device_id_type=MESH,
            ).start()
            return carry

        lax.fori_loop(0, TILES - 1, to_tiles, 0)
        sent_all.append((g_recv.at[it], base))
        if it < ITERS - 1:
            exch[it + 1, OWN] = delta
            around = up_and_dn(exch.at[it + 1])
            for one in around:
                one.wait_recv()
        else:
            for one in levels:
                one.wait()
            total_before, total_change = back[...] + levels_total(0), levels_total(1)
        pltpu.make_async_copy(g_recv.at[it], g_recv.at[it], recv_sem.at[base]).wait()
        both = both + jnp.sum(g_recv[it], axis=0)
        norm = jnp.sum(jnp.where(lane < 64, both, 0.0), axis=1, keepdims=True)
        curv = jnp.sum(jnp.where(lane < 64, 0.0, both), axis=1, keepdims=True)
        step = norm / (norm + curv)
        state = state - step * grad
        if it < ITERS - 1:
            smoothed = smoothed - step * change
    inc_out[...] = total_before - step.reshape(1, 1, 1) * total_change
    for m in range(2):
        state_out[m * 128 : m * 128 + 128, :] = state[:, m * 128 : m * 128 + 128].T
    for one in sent:
        one.wait_send()
    for ref, i in sent_all:
        pltpu.make_async_copy(ref, ref, send_sem.at[i]).wait()


def per_device(perturbations, control, background, obs_cell, huber_flag, innovation, precision):
    ky, kv = row_matrices()
    kx, sel = column_matrices(), row_selection()
    kxs = np.zeros((3, 256, 128), BF16)
    kxs[:, :, 0:48] = stack(kx[:, :, 128:144], 2)
    args = (
        perturbations.reshape(1280, 128), control.reshape(256, 128), background.reshape(5, 16, 128),
        obs_cell, huber_flag, innovation, precision,
        jnp.asarray(stack(ky, 1)), jnp.asarray(stack(kv[:, :256], 1)), jnp.asarray(stack(kv[:, 256:], 1)),
        jnp.asarray(stack(kx[:, :, :128], 2)), jnp.asarray(kxs), jnp.asarray(sel),
    )
    i32 = jnp.int32
    inc, state = pl.pallas_call(
        kernel,
        out_shape=(jax.ShapeDtypeStruct((5, 16, 128), F32), jax.ShapeDtypeStruct((256, 128), F32)),
        in_specs=[pl.BlockSpec(memory_space=pl.ANY)] * len(args),
        out_specs=(pl.BlockSpec(memory_space=pltpu.VMEM),) * 2,
        scratch_shapes=[
            pltpu.VMEM((1280, 128), BF16),
            pltpu.VMEM((256, 128), F32),
            pltpu.VMEM((5, 16, 128), F32),
            pltpu.VMEM((3, 32, 128), i32),
            pltpu.VMEM((3, 32, 128), i32),
            pltpu.VMEM((3, 32, 128), F32),
            pltpu.VMEM((3, 32, 128), F32),
            pltpu.VMEM((1152, 256), BF16),
            pltpu.VMEM((768, 256), BF16),
            pltpu.VMEM((768, 256), BF16),
            pltpu.VMEM((256, 384), BF16),
            pltpu.VMEM((256, 128), BF16),
            pltpu.VMEM((256, 256), F32),
            pltpu.VMEM((3, 256, 4096), BF16),
            pltpu.VMEM((640, 256), BF16),
            pltpu.VMEM((256, 256), BF16),
            pltpu.VMEM((256, 4096), BF16),
            pltpu.VMEM((640, 4096), F32),
            pltpu.VMEM((3, 2, 32, 128), F32),
            pltpu.VMEM((3, 32, 128), F32),
            pltpu.VMEM((256, 384), F32),
            pltpu.VMEM((ITERS, 3, 32, 128), F32),
            pltpu.VMEM((2, 128, 256), F32),
            pltpu.VMEM((32, 256), F32),
            pltpu.VMEM((ITERS, 2, 128, 256), F32),
            pltpu.VMEM((2, 128, 128), F32),
            pltpu.VMEM((2, 2, 8, 128), F32),
            pltpu.VMEM((2, 128, 128), F32),
            pltpu.VMEM((2, 4, 8, 128), F32),
            pltpu.VMEM((ITERS + 1, 40, 128), F32),
            pltpu.VMEM((ITERS + 1, MEM - 1, 40, 128), F32),
            pltpu.VMEM((ITERS, 2, 16, 384), F32),
            pltpu.VMEM((ITERS, 2, 16, 384), F32),
            pltpu.VMEM((ITERS, 1, 128), F32),
            pltpu.VMEM((ITERS, TILES - 1, 1, 128), F32),
            pltpu.VMEM((2, MEM, 5, 16, 128), F32),
            pltpu.VMEM((2, MEM - 1, 5, 16, 128), F32),
            pltpu.SemaphoreType.DMA((13,)),
            pltpu.SemaphoreType.DMA((40,)),
            pltpu.SemaphoreType.DMA((40,)),
            pltpu.SemaphoreType.REGULAR((2,)),
        ],
        compiler_params=pltpu.CompilerParams(collective_id=0, has_side_effects=True, vmem_limit_bytes=63 * 2**20 + 2**19),
    )(*args)
    return inc.reshape(background.shape), state.reshape(control.shape)


def solution(mesh):
    grid = P("mem", None, "gy", "gx")
    table = P("gy", "gx")
    return jax.shard_map(
        per_device,
        mesh=mesh,
        in_specs=(P("mem", None, None, "gy", "gx"), grid, P(None, "mem", "gy", "gx"), table, table, table, table),
        out_specs=(P(None, "mem", "gy", "gx"), grid),
        check_vma=False,
    )
```

time: 109 us -> 95.7 us (0.88)
  Pallas kernels: 105 us -> 91.9 us
  other arithmetic: 2.98 us -> 0 us
  local copies, waits for them, and re-layouts: 0.01 us -> 2.97 us
    pallas_call x1, Pallas kernels: 105 us -> 91.9 us  [per_device(): pl.pallas_call(kernel, out_shape=(jax.ShapeDtypeStruct((5, 16, 128), F32)...]
    unnamed x4 -> x2, local copies, waits for them, and re-layouts: 0.01 us -> 2.97 us
    sub x1 -> x0, other arithmetic: 1.57 us -> none  [per_device(): control - change.reshape(control.shape)]
    add x1 -> x0, other arithmetic: 1.4 us -> none  [per_device(): background + inc.reshape(background.shape)]
where the time goes in v2:
time: 95.7 us; the launch traced here: 95.5 us
  Pallas kernels  91.9 us (96%)
  local copies, waits for them, and re-layouts  2.97 us (3%)
    pallas_call x1, Pallas kernels, per_device(): pl.pallas_call(kernel, out_shape=(jax.ShapeDtypeStruct((5, 16, 128), F32)...  91.9 us
    unnamed x2, local copies, waits for them, and re-layouts  2.97 us

profile of v2, /device:TPU:1, one launch (start us, length us, event | category | flops | bytes accessed | tf_op | source)
XLA Modules:
  0.0 95.5 jit_solution(6439587262900244327)
XLA Ops:
  0.6 91.9 %shard_map.140 = (f32[5,16,128]{2,1,0:T(8,128)}, f32[256,128]{1,0:T(8,128)}) custom-call(bf16[1280,128]{1,0:T(8,128)(2,1)} %bitcast.5, f32[256,128]{1,0:T(8,128)} %bitcast.6, f32[5,16,128]{2,1,0:T(8,128)} %bitcast.9, s32[32,128]{1,0:T(8,128)} %cell_in.1, s32[32,128]{1,0:T(8,128)} %flag_in.1, f32[32,128]{1,0:T(8,128)} %innov_in.1, f32[32,128]{1,0:T(8,128)} %prec_in.1, ...), custom_call_target="tpu_custom_call" | custom-call | tf_op jit(solution)/shard_map/pallas_call | solution.py:470
  92.5 1.4 %copy.17 = f32[5,2,8,128]{3,2,1,0:T(8,128)} copy(f32[5,2,8,128]{3,2,1,0:T(8,128)} %bitcast.8) | data formatting | bytes 81920
  93.9 1.6 %copy.18 = f32[2,16,8,128]{3,2,1,0:T(8,128)} copy(f32[2,16,8,128]{3,2,1,0:T(8,128)} %bitcast.7) | data formatting | bytes 262144

commit v3 on v2

--- a/solution.py
+++ b/solution.py
@@ -13,6 +13,10 @@
 MEM, GY, GX = 8, 4, 16
 TILES = GY * GX
 ITERS = 2
+FAR_FIRST = sorted(
+    ((rows, cols) for rows in range(GY) for cols in range(GX) if rows or cols),
+    key=lambda at: -(4 * min(at[0], GY - at[0]) + min(at[1], GX - at[1]) / 4),
+)
 UP, OWN, DN = 0, 1, 2
 LF, RT = 0, 1
 
@@ -107,13 +111,13 @@
     return jnp.dot(stacked, jnp.concatenate(parts, axis=0), preferred_element_type=F32)
 
 
-def table_rows(body):
+def table_rows(body, first=0, last=8):
     def four(c, carry):
         for k in range(4):
             body(pl.ds(c * 4 + k, 1), pl.ds(pl.multiple_of(c * 512 + k * 128, 128), 128))
         return carry
 
-    lax.fori_loop(0, 8, four, 0)
+    lax.fori_loop(first, last, four, 0)
 
 
 def build_onehot(cell, onehot, t):
@@ -163,7 +167,7 @@
         total = jnp.where(index == (cell[OWN, r, :] & 63), total, 0.0)
         out[r, :] = jnp.sum(total, axis=0, keepdims=True)
 
-    table_rows(body)
+    return body
 
 
 def spread(t, q, cell, onehot, po, values, w):
@@ -187,6 +191,27 @@
             )
 
 
+def spread_edges(t, q, cell, onehot, po, values, edge):
+    index = lax.broadcasted_iota(jnp.int32, (8, 128), 0)
+
+    def body(r, lanes):
+        column = cell[t, r, :] & 63
+        for m in range(2):
+            value = po[t, m, r, :] * q[r, :]
+            hi = value.astype(BF16).astype(F32)
+            for side in range(2):
+                mine = index + 56 * side == column
+                both = jnp.concatenate([jnp.where(mine, hi, 0.0), jnp.where(mine, value - hi, 0.0)], axis=0)
+                values[side * 32 + m * 16 : side * 32 + m * 16 + 16, lanes] = both.astype(BF16)
+
+    table_rows(body)
+    got = lax.dot_general(values[...], onehot[t], (((1,), (1,)), ((), ())), preferred_element_type=F32)
+    for side in range(2):
+        for m in range(2):
+            block = got[side * 32 + m * 16 : side * 32 + m * 16 + 16, side * 128 : side * 128 + 128]
+            edge[side, m * 8 : m * 8 + 8, t * 128 : t * 128 + 128] = block[0:8] + block[8:16]
+
+
 def member_part(field, pert, out):
     turned = [field[:, m * 128 : m * 128 + 128].T for m in range(2)]
     for v in range(5):
@@ -199,8 +224,8 @@
     pert_in, ctrl_in, back_in, cell_in, flag_in, innov_in, prec_in, ky_in, kvo_in, kvh_in, kxo_in, kxs_in, sel_in,
     inc_out, state_out,
     pert, ctrl, back, cell, flag, innov, prec, ky, kvo, kvh, kxo, kxs, sel,
-    onehot, table, left, values, got, po, q, w, exch, part, edges, fields,
-    v_pack, v_edge, v_rows, v_strip, h_send, h_recv, w_send, w_recv, g_send, g_recv, r_send, r_recv,
+    onehot, table, left, values, edge_values, got, po, q, w, exch, part, edges, fields,
+    v_pack, v_edge, v_rows, v_strip, h_send, h_recv, h_recv_b, w_send, w_recv, g_send, g_recv, r_send, r_recv,
     local_sem, send_sem, recv_sem, far_sem,
 ):
     me_m, me_y, me_x = lax.axis_index("mem"), lax.axis_index("gy"), lax.axis_index("gx")
@@ -209,12 +234,6 @@
 
     def member_peer(i):
         return {"mem": lax.rem(me_m + i, MEM)}
-
-    def tile_peer(i):
-        return {
-            "gy": lax.rem(me_y + lax.rem(i // GX + 1, GY), GY),
-            "gx": lax.rem(me_x + lax.rem(lax.rem(i, GX) + 1, GX), GX),
-        }
 
     place = jnp.where(me_x == 0, 0, jnp.where(me_x == GX - 1, 2, 1))
     loads = [
@@ -318,11 +337,25 @@
     strips = times_matrix(jnp.concatenate(near, axis=0), kvo[...]) + times_matrix(jnp.concatenate(far, axis=0), kvh[...])
     smoothed = matrix_times(kxo[0:128, :], rows_v) + matrix_times(kxs[0:128, :], strips)
 
-    def members_total(phase):
-        out = h_send[phase]
-        for i in range(MEM - 1):
-            out += h_recv[phase, i]
-        return out
+    def sum_members(body, phase, norm):
+        table_rows(body, 0, 4)
+        first_half = to_members(lambda i: h_send.at[phase, pl.ds(0, 16)], h_recv.at[phase])
+        h_send[phase, 32:40, :] = norm
+        table_rows(body, 4, 8)
+        second_half = to_members(lambda i: h_send.at[phase, pl.ds(16, 24)], h_recv_b.at[phase])
+
+        def total():
+            first_half.wait()
+            one = h_send[phase, 0:16, :]
+            for i in range(MEM - 1):
+                one += h_recv[phase, i]
+            second_half.wait()
+            two = h_send[phase, 16:40, :]
+            for i in range(MEM - 1):
+                two += h_recv_b[phase, i]
+            return jnp.concatenate([one, two[0:16]], axis=0), two[16:24]
+
+        return total
 
     def levels_total(k):
         out = r_send[k, me_m]
@@ -330,15 +363,12 @@
             out += r_recv[k, i]
         return out
 
-    observe(smoothed, left, cell, onehot, got, po, h_send.at[0])
-    h_send[0, 32:40, :] = jnp.zeros((8, 128), F32)
-    arrived = to_members(lambda i: h_send.at[0], h_recv.at[0])
+    total = sum_members(observe(smoothed, left, cell, onehot, got, po, h_send.at[0]), 0, jnp.zeros((8, 128), F32))
     for one in tables[0:2]:
         one.wait_recv()
     build_onehot(cell, onehot, UP)
     build_onehot(cell, onehot, DN)
-    arrived.wait()
-    exch[0, OWN] = members_total(0)[0:32]
+    exch[0, OWN] = total()[0]
     around = up_and_dn(exch.at[0])
     pl.semaphore_wait(far_sem.at[0], 2)
     for offset in (4, GX - 4):
@@ -375,14 +405,16 @@
             inverse_t = terms(t, seen)
             if t == OWN:
                 inverse = inverse_t
-            spread(t, q.at[t], cell, onehot, po, values, w)
-        for m in range(2):
-            w_send[it, 0, m * 8 : m * 8 + 8, :] = w[m * 128 : m * 128 + 8, :]
-            w_send[it, 1, m * 8 : m * 8 + 8, :] = w[m * 128 + 120 : m * 128 + 128, :]
+            spread_edges(t, q.at[t], cell, onehot, po, edge_values, w_send.at[it])
+            if it == 0 and t == OWN:
+                spread(t, q.at[t], cell, onehot, po, values, w)
         sides = [copy(w_send.at[it, 0], w_recv.at[it, RT], lf), copy(w_send.at[it, 1], w_recv.at[it, LF], rt)]
         if it == ITERS - 1:
             member_part(smoothed, pert, r_send.at[0])
             levels.append(to_members(lambda i: r_send.at[0, lax.rem(me_m + i, MEM)], r_recv.at[0]))
+        for t in (OWN, UP, DN):
+            if it > 0 or t != OWN:
+                spread(t, q.at[t], cell, onehot, po, values, w)
         once, twice = x_stage(times_matrix(w[...], ky[...]), 128)
         part[0] = matrix_times(kxo[0:128, :], once)
         part[1] = matrix_times(kxo[128:256, :], twice)
@@ -395,17 +427,14 @@
         fields[it, 1] = matrix_times(kxs[128:256, :], edge_twice)
         grad = state + (part[0] + fields[it, 0])
         change = smoothed + (part[1] + fields[it, 1])
-        observe(change, left, cell, onehot, got, po, h_send.at[it + 1])
+        body = observe(change, left, cell, onehot, got, po, h_send.at[it + 1])
         norm = jnp.sum((grad * grad).reshape(16, 8, 256), axis=0)
-        h_send[it + 1, 32:40, :] = norm[:, 0:128] + norm[:, 128:256]
-        arrived = to_members(lambda i: h_send.at[it + 1], h_recv.at[it + 1])
+        total = sum_members(body, it + 1, norm[:, 0:128] + norm[:, 128:256])
         if it == ITERS - 1:
             member_part(change, pert, r_send.at[1])
             levels.append(to_members(lambda i: r_send.at[1, lax.rem(me_m + i, MEM)], r_recv.at[1]))
-        arrived.wait()
-        totals = members_total(it + 1)
-        delta = totals[0:32]
-        norm = jnp.sum(totals[32:40], axis=0, keepdims=True)
+        delta, norm = total()
+        norm = jnp.sum(norm, axis=0, keepdims=True)
         curv = jnp.sum(inverse * delta * delta, axis=0, keepdims=True)
         norm = norm + pltpu.roll(norm, 64, 1)
         curv = curv + pltpu.roll(curv, 64, 1)
@@ -416,18 +445,15 @@
         base = used[0]
         used[0] += 1
 
-        def to_tiles(i, carry):
+        for i, (rows, cols) in enumerate(FAR_FIRST):
             pltpu.make_async_remote_copy(
                 src_ref=g_send.at[it],
                 dst_ref=g_recv.at[it, i],
                 send_sem=send_sem.at[base],
                 recv_sem=recv_sem.at[base],
-                device_id=tile_peer(i),
+                device_id={"gy": lax.rem(me_y + rows, GY), "gx": lax.rem(me_x + cols, GX)},
                 device_id_type=MESH,
             ).start()
-            return carry
-
-        lax.fori_loop(0, TILES - 1, to_tiles, 0)
         sent_all.append((g_recv.at[it], base))
         if it < ITERS - 1:
             exch[it + 1, OWN] = delta
@@ -438,17 +464,18 @@
             for one in levels:
                 one.wait()
             total_before, total_change = back[...] + levels_total(0), levels_total(1)
+            turned = [[x[:, m * 128 : m * 128 + 128].T for m in range(2)] for x in (state, grad)]
         pltpu.make_async_copy(g_recv.at[it], g_recv.at[it], recv_sem.at[base]).wait()
         both = both + jnp.sum(g_recv[it], axis=0)
         norm = jnp.sum(jnp.where(lane < 64, both, 0.0), axis=1, keepdims=True)
         curv = jnp.sum(jnp.where(lane < 64, 0.0, both), axis=1, keepdims=True)
         step = norm / (norm + curv)
-        state = state - step * grad
         if it < ITERS - 1:
+            state = state - step * grad
             smoothed = smoothed - step * change
     inc_out[...] = total_before - step.reshape(1, 1, 1) * total_change
     for m in range(2):
-        state_out[m * 128 : m * 128 + 128, :] = state[:, m * 128 : m * 128 + 128].T
+        state_out[m * 128 : m * 128 + 128, :] = turned[0][m] - step * turned[1][m]
     for one in sent:
         one.wait_send()
     for ref, i in sent_all:
@@ -490,6 +517,7 @@
             pltpu.VMEM((640, 256), BF16),
             pltpu.VMEM((256, 256), BF16),
             pltpu.VMEM((256, 4096), BF16),
+            pltpu.VMEM((64, 4096), BF16),
             pltpu.VMEM((640, 4096), F32),
             pltpu.VMEM((3, 2, 32, 128), F32),
             pltpu.VMEM((3, 32, 128), F32),
@@ -503,7 +531,8 @@
             pltpu.VMEM((2, 128, 128), F32),
             pltpu.VMEM((2, 4, 8, 128), F32),
             pltpu.VMEM((ITERS + 1, 40, 128), F32),
-            pltpu.VMEM((ITERS + 1, MEM - 1, 40, 128), F32),
+            pltpu.VMEM((ITERS + 1, MEM - 1, 16, 128), F32),
+            pltpu.VMEM((ITERS + 1, MEM - 1, 24, 128), F32),
             pltpu.VMEM((ITERS, 2, 16, 384), F32),
             pltpu.VMEM((ITERS, 2, 16, 384), F32),
             pltpu.VMEM((ITERS, 1, 128), F32),

time: 95.7 us -> 93.6 us (0.978)
  Pallas kernels: 91.9 us -> 89.8 us
    pallas_call x1, Pallas kernels: 91.9 us -> 89.8 us  [per_device(): pl.pallas_call(kernel, out_shape=(jax.ShapeDtypeStruct((5, 16, 128), F32)...]
where the time goes in v3:
time: 93.6 us; the launch traced here: 93.4 us
  Pallas kernels  89.8 us (96%)
  local copies, waits for them, and re-layouts  2.97 us (3%)
    pallas_call x1, Pallas kernels, per_device(): pl.pallas_call(kernel, out_shape=(jax.ShapeDtypeStruct((5, 16, 128), F32)...  89.8 us
    unnamed x2, local copies, waits for them, and re-layouts  2.97 us

profile of v3, /device:TPU:1, one launch (start us, length us, event | category | flops | bytes accessed | tf_op | source)
XLA Modules:
  0.0 93.4 jit_solution(6838218975839625040)
XLA Ops:
  0.6 89.8 %shard_map.140 = (f32[5,16,128]{2,1,0:T(8,128)}, f32[256,128]{1,0:T(8,128)}) custom-call(bf16[1280,128]{1,0:T(8,128)(2,1)} %bitcast.5, f32[256,128]{1,0:T(8,128)} %bitcast.6, f32[5,16,128]{2,1,0:T(8,128)} %bitcast.9, s32[32,128]{1,0:T(8,128)} %cell_in.1, s32[32,128]{1,0:T(8,128)} %flag_in.1, f32[32,128]{1,0:T(8,128)} %innov_in.1, f32[32,128]{1,0:T(8,128)} %prec_in.1, ...), custom_call_target="tpu_custom_call" | custom-call | tf_op jit(solution)/shard_map/pallas_call | solution.py:497
  90.4 1.4 %copy.17 = f32[5,2,8,128]{3,2,1,0:T(8,128)} copy(f32[5,2,8,128]{3,2,1,0:T(8,128)} %bitcast.8) | data formatting | bytes 81920
  91.8 1.6 %copy.18 = f32[2,16,8,128]{3,2,1,0:T(8,128)} copy(f32[2,16,8,128]{3,2,1,0:T(8,128)} %bitcast.7) | data formatting | bytes 262144

commit v4 on v3

--- a/solution.py
+++ b/solution.py
@@ -480,6 +480,15 @@
         one.wait_send()
     for ref, i in sent_all:
         pltpu.make_async_copy(ref, ref, send_sem.at[i]).wait()
+
+
+def deliver(inc_in, state_in, inc_out, state_out, sem):
+    parts = [(inc_in, inc_out), (state_in.at[0:128], state_out.at[0:128]), (state_in.at[128:256], state_out.at[128:256])]
+    copies = [pltpu.make_async_copy(src, dst, sem.at[i]) for i, (src, dst) in enumerate(parts)]
+    for one in copies:
+        one.start()
+    for one in copies:
+        one.wait()
 
 
 def per_device(perturbations, control, background, obs_cell, huber_flag, innovation, precision):
@@ -546,6 +555,14 @@
         ],
         compiler_params=pltpu.CompilerParams(collective_id=0, has_side_effects=True, vmem_limit_bytes=63 * 2**20 + 2**19),
     )(*args)
+    inc, state = pl.pallas_call(
+        deliver,
+        out_shape=(jax.ShapeDtypeStruct(inc.shape, F32), jax.ShapeDtypeStruct(state.shape, F32)),
+        in_specs=[pl.BlockSpec(memory_space=pl.ANY)] * 2,
+        out_specs=(pl.BlockSpec(memory_space=pl.ANY),) * 2,
+        scratch_shapes=[pltpu.SemaphoreType.DMA((3,))],
+        compiler_params=pltpu.CompilerParams(vmem_limit_bytes=63 * 2**20 + 2**19),
+    )(inc, state)
     return inc.reshape(background.shape), state.reshape(control.shape)
 
 

time: 93.6 us -> 97 us (1.036)
  Pallas kernels: 89.8 us -> 96.1 us
  local copies, waits for them, and re-layouts: 2.97 us -> 0 us
    pallas_call x0 -> x1, Pallas kernels: none -> 6.34 us  [per_device(): pl.pallas_call(deliver, out_shape=(jax.ShapeDtypeStruct(inc.shape, F32),...]
    unnamed x2 -> x0, local copies, waits for them, and re-layouts: 2.97 us -> none
where the time goes in v4:
time: 97 us; the launch traced here: 96.9 us
  Pallas kernels  96.1 us (99%)
    pallas_call x1, Pallas kernels, per_device(): pl.pallas_call(kernel, out_shape=(jax.ShapeDtypeStruct((5, 16, 128), F32)...  89.8 us
    pallas_call x1, Pallas kernels, per_device(): pl.pallas_call(deliver, out_shape=(jax.ShapeDtypeStruct(inc.shape, F32),...  6.34 us

profile of v4, /device:TPU:1, one launch (start us, length us, event | category | flops | bytes accessed | tf_op | source)
XLA Modules:
  0.0 96.9 jit_solution(8901861877596833997)
XLA Ops:
  0.6 89.8 %shard_map.140 = (f32[5,16,128]{2,1,0:T(8,128)}, f32[256,128]{1,0:T(8,128)}) custom-call(bf16[1280,128]{1,0:T(8,128)(2,1)} %bitcast.5, f32[256,128]{1,0:T(8,128)} %bitcast.6, f32[5,16,128]{2,1,0:T(8,128)} %bitcast.7, s32[32,128]{1,0:T(8,128)} %cell_in.1, s32[32,128]{1,0:T(8,128)} %flag_in.1, f32[32,128]{1,0:T(8,128)} %innov_in.1, f32[32,128]{1,0:T(8,128)} %prec_in.1, ...), custom_call_target="tpu_custom_call" | custom-call | tf_op jit(solution)/shard_map/pallas_call | solution.py:506
  90.4 6.3 %shard_map.141 = (f32[5,16,128]{2,1,0:T(8,128)}, f32[256,128]{1,0:T(8,128)}) custom-call(f32[5,16,128]{2,1,0:T(8,128)} %get-tuple-element.6.inc_in, f32[256,128]{1,0:T(8,128)} %get-tuple-element.7.state_in), custom_call_target="tpu_custom_call" | custom-call | tf_op jit(solution)/shard_map/pallas_call | solution.py:558

commit v5 on v3

--- a/solution.py
+++ b/solution.py
@@ -480,6 +480,11 @@
         one.wait_send()
     for ref, i in sent_all:
         pltpu.make_async_copy(ref, ref, send_sem.at[i]).wait()
+
+
+def deliver(inc_in, state_in, inc_out, state_out):
+    inc_out[...] = inc_in[...]
+    state_out[...] = state_in[...]
 
 
 def per_device(perturbations, control, background, obs_cell, huber_flag, innovation, precision):
@@ -546,6 +551,13 @@
         ],
         compiler_params=pltpu.CompilerParams(collective_id=0, has_side_effects=True, vmem_limit_bytes=63 * 2**20 + 2**19),
     )(*args)
+    inc, state = pl.pallas_call(
+        deliver,
+        out_shape=(jax.ShapeDtypeStruct(inc.shape, F32), jax.ShapeDtypeStruct(state.shape, F32)),
+        in_specs=[pl.BlockSpec(memory_space=pltpu.VMEM)] * 2,
+        out_specs=(pl.BlockSpec(memory_space=pltpu.VMEM),) * 2,
+        compiler_params=pltpu.CompilerParams(vmem_limit_bytes=63 * 2**20 + 2**19),
+    )(inc, state)
     return inc.reshape(background.shape), state.reshape(control.shape)
 
 

time: 93.6 us -> 92.2 us (0.985)
  local copies, waits for them, and re-layouts: 2.97 us -> 0 us
  Pallas kernels: 89.8 us -> 91.4 us
    unnamed x2 -> x0, local copies, waits for them, and re-layouts: 2.97 us -> none
    pallas_call x0 -> x1, Pallas kernels: none -> 1.6 us  [per_device(): pl.pallas_call(deliver, out_shape=(jax.ShapeDtypeStruct(inc.shape, F32),...]
where the time goes in v5:
time: 92.2 us; the launch traced here: 92 us
  Pallas kernels  91.4 us (99%)
    pallas_call x1, Pallas kernels, per_device(): pl.pallas_call(kernel, out_shape=(jax.ShapeDtypeStruct((5, 16, 128), F32)...  89.8 us

profile of v5, /device:TPU:1, one launch (start us, length us, event | category | flops | bytes accessed | tf_op | source)
XLA Modules:
  0.0 92.0 jit_solution(8800719079953955980)
XLA Ops:
  0.6 89.8 %shard_map.140 = (f32[5,16,128]{2,1,0:T(8,128)}, f32[256,128]{1,0:T(8,128)}) custom-call(bf16[1280,128]{1,0:T(8,128)(2,1)} %bitcast.5, f32[256,128]{1,0:T(8,128)} %bitcast.6, f32[5,16,128]{2,1,0:T(8,128)} %bitcast.7, s32[32,128]{1,0:T(8,128)} %cell_in.1, s32[32,128]{1,0:T(8,128)} %flag_in.1, f32[32,128]{1,0:T(8,128)} %innov_in.1, f32[32,128]{1,0:T(8,128)} %prec_in.1, ...), custom_call_target="tpu_custom_call" | custom-call | tf_op jit(solution)/shard_map/pallas_call | solution.py:502
  90.4 1.6 %shard_map.141 = (f32[5,16,128]{2,1,0:T(8,128)}, f32[256,128]{1,0:T(8,128)}) custom-call(f32[5,16,128]{2,1,0:T(8,128)} %get-tuple-element.6.inc_in, f32[256,128]{1,0:T(8,128)} %get-tuple-element.7.state_in), custom_call_target="tpu_custom_call" | custom-call | tf_op jit(solution)/shard_map/pallas_call | solution.py:554

commit v6 on v5

--- a/solution.py
+++ b/solution.py
@@ -409,9 +409,6 @@
             if it == 0 and t == OWN:
                 spread(t, q.at[t], cell, onehot, po, values, w)
         sides = [copy(w_send.at[it, 0], w_recv.at[it, RT], lf), copy(w_send.at[it, 1], w_recv.at[it, LF], rt)]
-        if it == ITERS - 1:
-            member_part(smoothed, pert, r_send.at[0])
-            levels.append(to_members(lambda i: r_send.at[0, lax.rem(me_m + i, MEM)], r_recv.at[0]))
         for t in (OWN, UP, DN):
             if it > 0 or t != OWN:
                 spread(t, q.at[t], cell, onehot, po, values, w)
@@ -431,6 +428,8 @@
         norm = jnp.sum((grad * grad).reshape(16, 8, 256), axis=0)
         total = sum_members(body, it + 1, norm[:, 0:128] + norm[:, 128:256])
         if it == ITERS - 1:
+            member_part(smoothed, pert, r_send.at[0])
+            levels.append(to_members(lambda i: r_send.at[0, lax.rem(me_m + i, MEM)], r_recv.at[0]))
             member_part(change, pert, r_send.at[1])
             levels.append(to_members(lambda i: r_send.at[1, lax.rem(me_m + i, MEM)], r_recv.at[1]))
         delta, norm = total()

time: 92.2 us -> 92.1 us (level)
  no operation moved by 1% of the time
where the time goes in v6:
time: 92.1 us; the launch traced here: 91.9 us
  Pallas kernels  91.3 us (99%)
    pallas_call x1, Pallas kernels, per_device(): pl.pallas_call(kernel, out_shape=(jax.ShapeDtypeStruct((5, 16, 128), F32)...  89.7 us

profile of v6, /device:TPU:1, one launch (start us, length us, event | category | flops | bytes accessed | tf_op | source)
XLA Modules:
  0.0 91.9 jit_solution(4230970980011713783)
XLA Ops:
  0.6 89.7 %shard_map.140 = (f32[5,16,128]{2,1,0:T(8,128)}, f32[256,128]{1,0:T(8,128)}) custom-call(bf16[1280,128]{1,0:T(8,128)(2,1)} %bitcast.5, f32[256,128]{1,0:T(8,128)} %bitcast.6, f32[5,16,128]{2,1,0:T(8,128)} %bitcast.7, s32[32,128]{1,0:T(8,128)} %cell_in.1, s32[32,128]{1,0:T(8,128)} %flag_in.1, f32[32,128]{1,0:T(8,128)} %innov_in.1, f32[32,128]{1,0:T(8,128)} %prec_in.1, ...), custom_call_target="tpu_custom_call" | custom-call | tf_op jit(solution)/shard_map/pallas_call | solution.py:501
  90.3 1.6 %shard_map.141 = (f32[5,16,128]{2,1,0:T(8,128)}, f32[256,128]{1,0:T(8,128)}) custom-call(f32[5,16,128]{2,1,0:T(8,128)} %get-tuple-element.6.inc_in, f32[256,128]{1,0:T(8,128)} %get-tuple-element.7.state_in), custom_call_target="tpu_custom_call" | custom-call | tf_op jit(solution)/shard_map/pallas_call | solution.py:553
